TPU v7x, 32 devices: a whole 2x2x4 slice. The times are simulated.
32 devices in a mesh: lon: 16 (over z, x, core), lat: 2 (over y).
Axes of the slice: x: 2, y: 2, z: 4, core: 2. Of those that a mesh axis runs over, the one named last changes fastest.
Arguments:
- adjoint_final: float32 [34, 256, 256], P(None, 'lon', 'lat'), may hold values from -6 to 6
- lon_courant: float32 [2, 34, 256, 256], P(None, None, 'lon', 'lat'), may hold values from -0.9 to 0.9
- lon_branch: int32 [2, 34, 256, 256], P(None, None, 'lon', 'lat'), may hold values from 0 to 2
- lat_courant: float32 [2, 34, 256, 256], P(None, None, 'lon', 'lat'), may hold values from -0.9 to 0.9
- lat_branch: int32 [2, 34, 256, 256], P(None, None, 'lon', 'lat'), may hold values from 0 to 2
- mixing: float32 [2, 33, 256, 256], P(None, None, 'lon', 'lat'), may hold values from 0.05 to 5
- region_map: int32 [256, 256], P('lon', 'lat'), may hold values from 0 to 8191
- region_order: int32 [8192], replicated, may hold values from 0 to 8191, each once
- prior_cov: float32 [32, 256, 256], P('lon'), may hold values from -0.4 to 0.4
Outputs:
- adjoint_start: float32 [34, 256, 256], P(None, 'lon', 'lat')
- flux_gradient: float32 [2, 8192], P(None, ('lon', 'lat'))
Inputs may be any that keep to these rules, and one draw needn't show every extreme that they name: `region_order`: each position appears once.
All inputs are finite; a program needn't handle non-finite values.
Results may differ from a plain program's by a relative error of at most 0.0003.
Values sent between devices are 32-bit elements; how exact they have to be, the bound alone decides.
A program may use at most 128 MiB of HBM per device.

v0:
```python
import functools
import math

import jax
import jax.numpy as jnp
import numpy as np
from jax import lax
from jax.experimental import pallas as pl
from jax.experimental.pallas import tpu as pltpu
from jax.sharding import PartitionSpec as P

MESH = pl.DeviceIdType.MESH
OWN = 8


def face_weights(courant, branch):
    lean_part = courant * (0.5 * (1.0 - jnp.abs(courant)))
    one_part = jnp.where(branch == 1, lean_part, 0.0)
    two_part = jnp.where(branch == 2, lean_part, 0.0)
    donor = courant - one_part + two_part
    left = courant > 0.0
    return (
        jnp.where(left, -two_part, 0.0),
        jnp.where(left, donor, one_part),
        jnp.where(left, one_part, donor),
        jnp.where(left, 0.0, -two_part),
    )


def kernel(
    nlon,
    nlat,
    width,
    adj_h,
    lonc_h,
    lonb_h,
    latc_h,
    latb_h,
    mix_h,
    cov_h,
    rmap_h,
    order_h,
    cos_h,
    out_ref,
    flux_ref,
    rmap_ref,
    order_ref,
    cos_ref,
    x_ref,
    mixv,
    latc,
    latb,
    lonc,
    lonb,
    covv,
    covh,
    covl,
    inv_ref,
    kin_ref,
    nr_ref,
    y_ref,
    ext,
    lw,
    pack_w,
    land_w,
    pack_a,
    land_a,
    raw_rows,
    rows_a,
    far_a,
    rows_w,
    hi_ref,
    lo_ref,
    cht,
    amat,
    pscr,
    send_ref,
    land,
    local_sem,
    send_sem,
    recv_sem,
    all_sem,
):
    steps, levels, rows, lanes = latc.shape
    count = nlon * nlat
    my_lon, my_lat = lax.axis_index("lon"), lax.axis_index("lat")
    me = my_lon * nlat + my_lat
    blk = covv.shape[0]

    def place(device):
        return (device // nlat, lax.rem(device, nlat))

    barrier = pltpu.get_barrier_semaphore()

    def fetch(src, dst, slot):
        copy = pltpu.make_async_copy(src, dst, local_sem.at[slot])
        copy.start()
        return copy

    get_mix, get_lat, get_lon = {}, {}, {}
    get_mix[1] = fetch(mix_h.at[1], mixv.at[1], 0)
    get_adj = fetch(adj_h, x_ref, 1)
    for s in (1, 0):
        at = 2 + 5 * (1 - s)
        get_lat[s] = (
            fetch(latc_h.at[s], latc.at[s], at),
            fetch(latb_h.at[s], latb.at[s], at + 1),
        )
        get_lon[s] = (
            fetch(lonc_h.at[s], lonc.at[s], at + 2),
            fetch(lonb_h.at[s], lonb.at[s], at + 3),
        )
        if s == 1:
            get_mix[0] = fetch(mix_h.at[0], mixv.at[0], at + 4)
    get_small = (
        fetch(rmap_h, rmap_ref, 11),
        fetch(order_h, order_ref, 12),
        fetch(cos_h.at[my_lat], cos_ref, 13),
    )
    get_cov = fetch(cov_h.at[(my_lat * width) // blk], covv, 14)

    far_first = jnp.where(my_lon >= nlon // 2, 1, 0)

    def greet(k, carry):
        device = far_first * k + (1 - far_first) * (count - 1 - k)

        @pl.when(device != me)
        def _():
            pl.semaphore_signal(barrier, inc=1, device_id=place(device), device_id_type=MESH)

        return carry

    lax.fori_loop(0, count, greet, 0)

    lane = lax.broadcasted_iota(jnp.int32, (rows, lanes), 1)
    pair = lane // 2
    even = lax.rem(lane, 2) == 0
    zero = jnp.zeros((rows, lanes), jnp.float32)

    def roll(value, shift):
        return pltpu.roll(value, shift, 1)

    def remote(src, dst, slot, device):
        copy = pltpu.make_async_remote_copy(
            src_ref=src,
            dst_ref=dst,
            send_sem=send_sem.at[slot],
            recv_sem=recv_sem.at[slot],
            device_id=device,
            device_id_type=MESH,
        )
        copy.start()
        return copy

    north = (my_lon, lax.rem(my_lat + 1, nlat))
    south = (my_lon, lax.rem(my_lat + nlat - 1, nlat))
    east = (lax.rem(my_lon + 1, nlon), my_lat)
    west = (lax.rem(my_lon + nlon - 1, nlon), my_lat)

    def coefficients(s):
        k = mixv[s, 0]
        inv = 1.0 / (1.0 + k)
        inv_ref[s, 0] = inv
        kin_ref[s, 0] = zero
        nr_ref[s, 0] = k * inv

        def body(level, ahead):
            lower, k = mixv[s, level - 1], mixv[s, level]
            inv = 1.0 / ((1.0 + k) + lower * (1.0 - ahead))
            inv_ref[s, level] = inv
            kin_ref[s, level] = lower * inv
            ahead = k * inv
            nr_ref[s, level] = ahead
            return ahead

        ahead = lax.fori_loop(1, levels - 1, body, k * inv, unroll=True)
        lower = mixv[s, levels - 2]
        inv = 1.0 / (1.0 + lower * (1.0 - ahead))
        inv_ref[s, levels - 1] = inv
        kin_ref[s, levels - 1] = lower * inv
        nr_ref[s, levels - 1] = zero

    def tail_head(value, level, tail, head):
        turned = roll(value, 2 * level + 2)
        return jnp.where(pair == level, turned, tail), jnp.where(pair == level + 1, turned, head)

    def solve(s):
        def up(level, carried):
            carried = x_ref[level] * inv_ref[s, level] + kin_ref[s, level] * carried
            y_ref[level] = carried
            return carried

        lax.fori_loop(0, levels, up, zero, unroll=True)

        def down(i, carry):
            value, tail, head = carry
            level = levels - 1 - i
            value = y_ref[level] + nr_ref[s, level] * value
            y_ref[level] = value
            raw_rows[0, pl.ds(2 * level, 2), :] = value[rows - 2 :]
            raw_rows[1, pl.ds(2 * level, 2), :] = value[:2]
            return (value,) + tail_head(value, level, tail, head)

        _, tail, head = lax.fori_loop(0, levels, down, (zero, zero, zero), unroll=True)
        head = roll(head, lanes - 2)
        for member, value in enumerate((tail, head)):
            pack_a[s, member, OWN : OWN + rows] = value
            at = 2 * levels + 2 * member
            rows_a[0, s, at : at + 2] = value[rows - 2 :]
            rows_a[1, s, at : at + 2] = value[:2]

    def pack_weights(s):
        def body(level, carry):
            ct, ch, bt, bh = carry
            ct, ch = tail_head(latc[s, level], level, ct, ch)
            both = (latc[s, level], latb[s, level].astype(jnp.float32))
            bt, bh = tail_head(both[1], level, bt, bh)
            for member in range(2):
                rows_w[0, s, member, pl.ds(2 * level, 2), :] = both[member][rows - 2 :]
                rows_w[1, s, member, pl.ds(2 * level, 2), :] = both[member][:2]
            return ct, ch, bt, bh

        ct, ch, bt, bh = lax.fori_loop(0, levels, body, (zero,) * 4, unroll=True)
        found = ((ct, bt), (roll(ch, lanes - 2), roll(bh, lanes - 2)))
        for end in range(2):
            for member in range(2):
                pack_w[end, s, member, OWN : OWN + rows] = found[end][member]
        for member in range(2):
            at = 2 * levels + 4 + 2 * member
            rows_a[0, s, at : at + 2] = found[1][member][rows - 2 :]
            rows_a[1, s, at : at + 2] = found[1][member][:2]

    def lat_rows(s):
        for side in range(2):
            rows_a[side, s, : 2 * levels] = lat_pass(
                raw_rows[side], rows_w[side, s, 0], rows_w[side, s, 1]
            )

    def lat_pass(a, courant, branch):
        at = lax.broadcasted_iota(jnp.int32, a.shape, 1)
        m2, m1, m0, p1 = face_weights(courant, branch)
        jump = jnp.where(at >= 1, a - roll(a, 1), 0.0)
        out = a + m0 * jump + roll(m1 * jump, lanes - 1)
        out = out + roll(jnp.where(at >= 2, m2 * jump, 0.0), lanes - 2)
        return out + roll(jnp.where(at <= lanes - 2, p1 * jump, 0.0), 1)

    def lat_inner(s):
        def body(level, carry):
            out = lat_pass(y_ref[level], latc[s, level], latb[s, level])
            ext[s, level, OWN : OWN + rows] = out
            return carry

        lax.fori_loop(0, levels, body, 0, unroll=True)

    def lat_edges(s):
        at = 2 * levels
        lane = lax.broadcasted_iota(jnp.int32, (rows + 2 * OWN, lanes), 1)
        even = lax.rem(lane, 2) == 0
        for side, where in enumerate((slice(OWN - 2, OWN), slice(OWN + rows, OWN + rows + 2))):
            for member in range(2):
                pack_a[s, member, where] = far_a[side, s, at + 2 * member : at + 2 * member + 2]
                far = at + 4 + 2 * member
                pack_w[1, s, member, where] = far_a[side, s, far : far + 2]
        tail, head = pack_a[s, 0], pack_a[s, 1]
        before, after = land_a[s, 0], land_a[s, 1]
        m2_after, m1_after, _, _ = face_weights(land_w[1, s, 0], land_w[1, s, 1])
        _, _, m0_head, p1_head = face_weights(pack_w[1, s, 0], pack_w[1, s, 1])
        _, _, _, p1_before = face_weights(land_w[0, s, 0], land_w[0, s, 1])
        jump = after - jnp.where(even, roll(tail, lanes - 1), roll(after, 1))
        top = m2_after * jump + roll(jnp.where(even, m1_after * jump, 0.0), 1)
        top = jnp.where(my_lat < nlat - 1, top, 0.0)
        jump = jnp.where(even, head - roll(before, lanes - 1), before - roll(before, 1))
        flux = jnp.where(even, p1_head, p1_before) * jump
        low = jnp.where(even, m0_head * jump + roll(flux, lanes - 1), roll(flux, 1))
        low = roll(jnp.where(my_lat > 0, low, 0.0), 2)
        first = lax.rem(lane, 4) < 2
        both = (jnp.where(first, top, low), jnp.where(first, low, top))
        edge = jnp.logical_or(lane < 2, lane >= lanes - 2)

        def body(m, carry):
            for odd in range(2):
                level = 2 * m + odd
                turned = jnp.where(edge, roll(both[odd], lanes - 2 - 2 * level), 0.0)
                ext[s, level, OWN : OWN + rows] += turned[OWN : OWN + rows]
                two = pl.ds(2 * level, 2)
                end = OWN + rows
                ext[s, level, OWN - 2 : OWN] = far_a[0, s, two, :] + turned[OWN - 2 : OWN]
                ext[s, level, end : end + 2] = far_a[1, s, two, :] + turned[end : end + 2]
            return carry

        lax.fori_loop(0, levels // 2, body, 0, unroll=True)

    def lon_own_weights(s):
        def body(level, carry):
            found = face_weights(
                lonc[s, level], lonb[s, level]
            )
            for member in range(4):
                lw[s, member, level, OWN : OWN + rows] = found[member]
            return carry

        lax.fori_loop(0, levels, body, 0, unroll=True)

    def lon_level(s, level):
        a = [ext[s, level, OWN + k : OWN + k + rows] for k in range(-2, 3)]
        w = [
            lw[s, member, level, OWN + 2 - member : OWN + 2 - member + rows]
            for member in range(4)
        ]
        out = a[2] + w[0] * (a[4] - a[3]) + w[1] * (a[3] - a[2])
        return out + w[2] * (a[2] - a[1]) + w[3] * (a[1] - a[0])

    def send_lon(s, base):
        end = OWN + rows
        return tuple(
            remote(
                lw.at[s, member, :, pl.ds(src, size), :],
                lw.at[s, member, :, pl.ds(dst, size), :],
                base + k,
                device,
            )
            for k, (member, src, dst, size, device) in enumerate(
                (
                    (0, OWN, end, 2, west),
                    (1, OWN, end, 1, west),
                    (3, end - 1, OWN - 1, 1, east),
                )
            )
        )

    def find_slots():
        order = order_ref[...]
        table = jnp.concatenate([order // 128, lax.rem(order, 128)], axis=0)
        table = table.astype(jnp.float32).astype(jnp.bfloat16)
        high = order.shape[0]
        down = lax.broadcasted_iota(jnp.int32, (lanes, lanes), 0)
        row_of = lax.broadcasted_iota(jnp.int32, (high, lanes), 0)
        for i in range(rows):
            region = rmap_ref[i : i + 1, :]
            hit = jnp.where(down == lax.rem(region, 128), 1.0, 0.0).astype(jnp.bfloat16)
            found = jnp.dot(table, hit, preferred_element_type=jnp.float32)
            here = row_of == region // 128
            hi = jnp.sum(jnp.where(here, found[:high], 0.0), axis=0, keepdims=True)
            lo = jnp.sum(jnp.where(here, found[high:], 0.0), axis=0, keepdims=True)
            hi_ref[i : i + 1, :] = hi
            cht[:, i * lanes : (i + 1) * lanes] = jnp.where(
                down.astype(jnp.float32) == lo, 1.0, 0.0
            ).astype(jnp.bfloat16)

    def regions(s, field):
        high = order_ref.shape[0]
        row_of = lax.broadcasted_iota(jnp.int32, (high, lanes), 0).astype(jnp.float32)
        lo_ref[...] = field
        for i in range(rows):
            here = row_of == hi_ref[i : i + 1, :]
            spread = jnp.where(here, lo_ref[i : i + 1, :], 0.0)
            coarse = spread.astype(jnp.bfloat16)
            fine = (spread - coarse.astype(jnp.float32)).astype(jnp.bfloat16)
            amat[:high, i * lanes : (i + 1) * lanes] = coarse
            amat[high:, i * lanes : (i + 1) * lanes] = fine
        sums = lax.dot_general(
            amat[...], cht[...], (((1,), (1,)), ((), ())), preferred_element_type=jnp.float32
        )
        pscr[...] = sums[:high] + sums[high:]
        for group in range(high // 2):
            send_ref[s, group] = pscr[2 * group : 2 * group + 2, :]

    get_mix[1].wait()
    coefficients(1)
    get_adj.wait()
    solve(1)
    for copy in get_lat[1]:
        copy.wait()
    pack_weights(1)
    lat_rows(1)
    for copy in get_lon[1]:
        copy.wait()
    lon_own_weights(1)
    pl.semaphore_wait(barrier, count - 1)

    turn = {1: lax.rem(my_lon + 1, nlon), -1: lax.rem(my_lon + nlon - 1, nlon)}
    own_rows, first, last_two = pl.ds(OWN, rows), pl.ds(OWN, 2), pl.ds(OWN + rows - 2, 2)
    low, high = pl.ds(OWN - 2, 2), pl.ds(OWN + rows, 2)

    def send_columns(source, target, base):
        copies = []
        for end in range(2):
            beside = (north, south)[end][1]
            for k, (lon, src, dst) in enumerate(
                (
                    (my_lon, own_rows, own_rows),
                    (turn[1], last_two, low),
                    (turn[-1], first, high),
                )
            ):
                copies.append(
                    remote(source(end, src), target(end, dst), base + 3 * end + k, (lon, beside))
                )
        return tuple(copies)

    def exchange(s, base):
        return (
            remote(rows_a.at[0, s], far_a.at[0, s], base, east),
            remote(rows_a.at[1, s], far_a.at[1, s], base + 1, west),
        ) + send_columns(
            lambda end, at: pack_a.at[s, end, at, :],
            lambda end, at: land_a.at[s, end, at, :],
            base + 2,
        )

    def send_lat_weights(s, base):
        return send_columns(
            lambda end, at: pack_w.at[end, s, :, at, :],
            lambda end, at: land_w.at[end, s, :, at, :],
            base,
        )

    def group_of(device):
        return (device * width) // blk

    def scatter(s):
        def body(k, carry):
            device = lax.rem(me + k, count)
            pltpu.make_async_remote_copy(
                src_ref=send_ref.at[s, group_of(device)],
                dst_ref=land.at[s, me],
                send_sem=all_sem.at[2 * s],
                recv_sem=all_sem.at[2 * s + 1],
                device_id=place(device),
                device_id_type=MESH,
            ).start()
            return carry

        lax.fori_loop(1, count, body, 0)
        land[s, me] = send_ref[s, group_of(me)]

    sent_a = {1: exchange(1, 0)}
    sent_w = {1: send_lat_weights(1, 16)}
    sent_lon = {1: send_lon(1, 28)}
    lat_inner(1)
    get_mix[0].wait()
    coefficients(0)
    for copy in get_lat[0]:
        copy.wait()
    pack_weights(0)
    sent_w[0] = send_lat_weights(0, 22)
    for copy in get_lon[0]:
        copy.wait()
    lon_own_weights(0)
    sent_lon[0] = send_lon(0, 31)
    for copy in get_small:
        copy.wait()
    cosine = cos_ref[...]
    find_slots()
    for copy in sent_a[1] + sent_w[1]:
        copy.wait_recv()
    lat_edges(1)
    for copy in sent_lon[1]:
        copy.wait_recv()

    def middle(level, carry):
        x_ref[level] = lon_level(1, level)
        return carry

    lax.fori_loop(0, levels, middle, 0, unroll=True)
    solve(0)
    lat_rows(0)
    sent_a[0] = exchange(0, 8)
    regions(1, x_ref[0] * cosine)
    scatter(1)
    lat_inner(0)
    get_cov.wait()
    covh[...] = covv[...].astype(jnp.bfloat16)
    covl[...] = (covv[...] - covh[...].astype(jnp.float32)).astype(jnp.bfloat16)
    for copy in sent_a[0] + sent_w[0]:
        copy.wait_recv()
    lat_edges(0)
    for copy in sent_lon[0]:
        copy.wait_recv()
    start = lon_level(0, 0)
    out_ref[0] = start
    regions(0, start * cosine)
    scatter(0)

    def last(level, carry):
        out_ref[level] = lon_level(0, level)
        return carry

    lax.fori_loop(1, levels, last, 0, unroll=True)
    for s in range(steps):
        for copy in sent_a[s] + sent_w[s] + sent_lon[s]:
            copy.wait_send()
    for s in range(steps):
        every = land.at[s, pl.ds(0, count - 1)]
        pltpu.make_async_copy(every, every, all_sem.at[2 * s]).wait()
        pltpu.make_async_copy(every, every, all_sem.at[2 * s + 1]).wait()
    totals = jnp.concatenate([jnp.sum(land[s], axis=0) for s in range(steps)], axis=0)
    coarse = totals.astype(jnp.bfloat16).astype(jnp.float32)
    both = jnp.concatenate([coarse, totals - coarse, jnp.zeros((8, lanes), jnp.float32)], axis=0)
    both = both.astype(jnp.bfloat16)
    half = blk // 2

    def product(at):
        found = jnp.dot(both, covh[at], preferred_element_type=jnp.float32)
        found = found + jnp.dot(both, covl[at], preferred_element_type=jnp.float32)
        return found[:4] + found[4:8]

    one, two = product(slice(0, half)), product(slice(half, blk))
    for s in range(steps):
        flux_ref[s : s + 1, :] = one[2 * s : 2 * s + 1] + two[2 * s + 1 : 2 * s + 2]


def per_device(
    nlon,
    nlat,
    adjoint_final,
    lon_courant,
    lon_branch,
    lat_courant,
    lat_branch,
    mixing,
    region_map,
    region_order,
    prior_cov,
):
    steps, levels, rows, lanes = lon_courant.shape
    regions = region_order.shape[0]
    blk = prior_cov.shape[1]
    width = regions // (nlon * nlat)
    lat_total = lanes * nlat
    lat_index = np.arange(lat_total, dtype=np.float32)
    angle = (lat_index + np.float32(0.5)) * np.float32(math.pi / lat_total)
    cosines = np.cos((angle - np.float32(0.5 * math.pi)).astype(np.float32))
    cosines = jnp.asarray(cosines.astype(np.float32).reshape(nlat, 1, lanes))
    f32, i32, b16 = jnp.float32, jnp.int32, jnp.bfloat16
    field = (levels, rows, lanes)
    tall = (levels, rows + 2 * OWN, lanes)
    vm = pltpu.VMEM
    scratch = [
        vm((rows, lanes), i32),
        vm((regions // 128, 128), i32),
        vm((1, lanes), f32),
        vm(field, f32),
        vm((steps, levels - 1, rows, lanes), f32),
        vm((steps,) + field, f32),
        vm((steps,) + field, i32),
        vm((steps,) + field, f32),
        vm((steps,) + field, i32),
        vm((blk, blk), f32),
        vm((blk, blk), b16),
        vm((blk, blk), b16),
        vm((steps,) + field, f32),
        vm((steps,) + field, f32),
        vm((steps,) + field, f32),
        vm(field, f32),
        vm((steps,) + tall, f32),
        vm((steps, 4) + tall, f32),
        vm((2, steps, 2, rows + 2 * OWN, lanes), f32),
        vm((2, steps, 2, rows + 2 * OWN, lanes), f32),
        vm((steps, 2, rows + 2 * OWN, lanes), f32),
        vm((steps, 2, rows + 2 * OWN, lanes), f32),
        vm((2, 2 * levels, lanes), f32),
        vm((2, steps, 2 * levels + 8, lanes), f32),
        vm((2, steps, 2 * levels + 8, lanes), f32),
        vm((2, steps, 2, 2 * levels, lanes), f32),
        vm((rows, lanes), f32),
        vm((rows, lanes), f32),
        vm((128, rows * lanes), b16),
        vm((2 * (regions // 128), rows * lanes), b16),
        vm((regions // 128, 128), f32),
        vm((steps, regions // blk, 2, 128), f32),
        vm((steps, nlon * nlat, 2, 128), f32),
        pltpu.SemaphoreType.DMA((15,)),
        pltpu.SemaphoreType.DMA((34,)),
        pltpu.SemaphoreType.DMA((34,)),
        pltpu.SemaphoreType.DMA((4,)),
    ]
    adjoint, flux = pl.pallas_call(
        functools.partial(kernel, nlon, nlat, width),
        out_shape=(
            pltpu.VMEM(field, f32),
            pltpu.VMEM((steps, blk), f32),
        ),
        in_specs=[pl.BlockSpec(memory_space=pltpu.HBM)] * 10,
        out_specs=(
            pl.BlockSpec(memory_space=pltpu.VMEM),
            pl.BlockSpec(memory_space=pltpu.VMEM),
        ),
        scratch_shapes=scratch,
        compiler_params=pltpu.CompilerParams(
            collective_id=0, has_side_effects=True, vmem_limit_bytes=61 * 1024 * 1024
        ),
    )(
        adjoint_final,
        lon_courant,
        lon_branch,
        lat_courant,
        lat_branch,
        mixing,
        prior_cov,
        region_map,
        region_order.reshape(regions // 128, 128),
        cosines,
    )
    if width < blk:
        start = lax.rem(lax.axis_index("lat") * width, blk)
        flux = lax.dynamic_slice_in_dim(flux, start, width, 1)
    return adjoint, flux


def solution(mesh):
    four = P(None, None, "lon", "lat")
    placed = (
        P(None, "lon", "lat"),
        four,
        four,
        four,
        four,
        four,
        P("lon", "lat"),
        P(),
        P("lon", None, None),
    )
    return jax.shard_map(
        functools.partial(per_device, mesh.shape["lon"], mesh.shape["lat"]),
        mesh=mesh,
        in_specs=placed,
        out_specs=(P(None, "lon", "lat"), P(None, ("lon", "lat"))),
        check_vma=False,
    )
```

profile of v0, /device:TPU:0, one launch (start us, length us, event | category | flops | bytes accessed | tf_op | source)
XLA Modules:
  0.0 23.8 jit_solution(15435862080889061438)
XLA Ops:
  0.6 21.8 %shard_map.113 = (f32[34,16,128]{2,1,0:T(8,128)S(1)}, f32[2,256]{1,0:T(2,128)S(1)}) custom-call(f32[34,16,128]{2,1,0:T(8,128)} %adj_h.1, f32[2,34,16,128]{3,2,1,0:T(8,128)} %lonc_h.1, s32[2,34,16,128]{3,2,1,0:T(8,128)} %lonb_h.1, f32[2,34,16,128]{3,2,1,0:T(8,128)} %latc_h.1, s32[2,34,16,128]{3,2,1,0:T(8,128)} %latb_h.1, f32[2,33,16,128]{3,2,1,0:T(8,128)} %mix_h.1, ...), custom_call_target="tpu_custom_call" | custom-call | tf_op jit(solution)/shard_map/pallas_call | solution.py:578
  22.5 0.7 %copy.14 = f32[34,16,128]{2,1,0:T(8,128)} copy(f32[34,16,128]{2,1,0:T(8,128)S(1)} %get-tuple-element.2) | data formatting | bytes 557056
  23.2 0.6 %copy.15 = f32[2,256]{1,0:T(2,128)} copy(f32[2,256]{1,0:T(2,128)S(1)} %get-tuple-element.3) | data formatting | bytes 4096
where the time goes:
time: 23.9 us; the launch traced here: 23.8 us
  Pallas kernels  21.8 us (91%)
  local copies, waits for them, and re-layouts  1.29 us (5%)
  between operations  0.64 us (3%)
    pallas_call x1, Pallas kernels, per_device(): pl.pallas_call(functools.partial(kernel, nlon, nlat, width), out_shape=(p...  21.8 us
    unnamed x2, local copies, waits for them, and re-layouts  1.29 us

commit v1 on v0

--- a/solution.py
+++ b/solution.py
@@ -41,6 +41,8 @@
     rmap_h,
     order_h,
     cos_h,
+    out_h,
+    flux_h,
     out_ref,
     flux_ref,
     rmap_ref,
@@ -69,11 +71,14 @@
     rows_a,
     far_a,
     rows_w,
-    hi_ref,
-    lo_ref,
+    ids,
+    beside,
+    lat_c,
+    lon_c,
+    bext,
+    hot,
     cht,
     amat,
-    pscr,
     send_ref,
     land,
     local_sem,
@@ -115,7 +120,7 @@
     get_small = (
         fetch(rmap_h, rmap_ref, 11),
         fetch(order_h, order_ref, 12),
-        fetch(cos_h.at[my_lat], cos_ref, 13),
+        fetch(cos_h, cos_ref, 13),
     )
     get_cov = fetch(cov_h.at[(my_lat * width) // blk], covv, 14)
 
@@ -140,7 +145,7 @@
     def roll(value, shift):
         return pltpu.roll(value, shift, 1)
 
-    def remote(src, dst, slot, device):
+    def remote(src, dst, slot, device, start=True):
         copy = pltpu.make_async_remote_copy(
             src_ref=src,
             dst_ref=dst,
@@ -149,7 +154,8 @@
             device_id=device,
             device_id_type=MESH,
         )
-        copy.start()
+        if start:
+            copy.start()
         return copy
 
     north = (my_lon, lax.rem(my_lat + 1, nlat))
@@ -328,42 +334,131 @@
             )
         )
 
-    def find_slots():
+    def find_slots(found_rows):
         order = order_ref[...]
         table = jnp.concatenate([order // 128, lax.rem(order, 128)], axis=0)
         table = table.astype(jnp.float32).astype(jnp.bfloat16)
         high = order.shape[0]
         down = lax.broadcasted_iota(jnp.int32, (lanes, lanes), 0)
         row_of = lax.broadcasted_iota(jnp.int32, (high, lanes), 0)
-        for i in range(rows):
-            region = rmap_ref[i : i + 1, :]
+        for i, region in found_rows:
             hit = jnp.where(down == lax.rem(region, 128), 1.0, 0.0).astype(jnp.bfloat16)
             found = jnp.dot(table, hit, preferred_element_type=jnp.float32)
             here = row_of == region // 128
             hi = jnp.sum(jnp.where(here, found[:high], 0.0), axis=0, keepdims=True)
             lo = jnp.sum(jnp.where(here, found[high:], 0.0), axis=0, keepdims=True)
-            hi_ref[i : i + 1, :] = hi
-            cht[:, i * lanes : (i + 1) * lanes] = jnp.where(
-                down.astype(jnp.float32) == lo, 1.0, 0.0
-            ).astype(jnp.bfloat16)
-
-    def regions(s, field):
+            at = slice(i * lanes, (i + 1) * lanes)
+            hot[:, at] = jnp.where(row_of.astype(jnp.float32) == hi, 1.0, 0.0).astype(jnp.bfloat16)
+            cht[:, at] = jnp.where(down.astype(jnp.float32) == lo, 1.0, 0.0).astype(jnp.bfloat16)
+
+    def regions(s, first, fields):
         high = order_ref.shape[0]
-        row_of = lax.broadcasted_iota(jnp.int32, (high, lanes), 0).astype(jnp.float32)
-        lo_ref[...] = field
-        for i in range(rows):
-            here = row_of == hi_ref[i : i + 1, :]
-            spread = jnp.where(here, lo_ref[i : i + 1, :], 0.0)
-            coarse = spread.astype(jnp.bfloat16)
-            fine = (spread - coarse.astype(jnp.float32)).astype(jnp.bfloat16)
-            amat[:high, i * lanes : (i + 1) * lanes] = coarse
-            amat[high:, i * lanes : (i + 1) * lanes] = fine
+        coarse = [field.astype(jnp.bfloat16).astype(jnp.float32) for field in fields]
+        fine = [field - part for field, part in zip(fields, coarse)]
+        at = first
+        for field in range(len(fields)):
+            for i in range(fields[field].shape[0]):
+                here = slice(at * lanes, (at + 1) * lanes)
+                for part, values in enumerate((coarse, fine)):
+                    value = jnp.broadcast_to(values[field][i : i + 1], (high, lanes))
+                    amat[part * high : (part + 1) * high, here] = hot[:, here] * value.astype(
+                        jnp.bfloat16
+                    )
+                at += 1
+        every = slice(first * lanes, at * lanes)
         sums = lax.dot_general(
-            amat[...], cht[...], (((1,), (1,)), ((), ())), preferred_element_type=jnp.float32
-        )
-        pscr[...] = sums[:high] + sums[high:]
+            amat[:, every],
+            cht[:, every],
+            (((1,), (1,)), ((), ())),
+            preferred_element_type=jnp.float32,
+        )
+        sums = sums[:high] + sums[high:]
         for group in range(high // 2):
-            send_ref[s, group] = pscr[2 * group : 2 * group + 2, :]
+            send_ref[group, 2 * s : 2 * s + 2, :] = sums[2 * group : 2 * group + 2]
+
+    tall_rows = rows + 2 * OWN
+    few = slice(OWN - 2, OWN + rows + 6)
+    has_north, has_south = my_lat < nlat - 1, my_lat > 0
+
+    def push_lat():
+        courant = jnp.where(jnp.logical_and(lane == 0, my_lat == 0), 0.0, latc[0, 0])
+        m2, m1, m0, p1 = face_weights(courant, latb[0, 0])
+        north_c = jnp.where(has_north, land_w[1, 0, 0, OWN : OWN + rows], 0.0)
+        n2, n1, n0, np1 = face_weights(north_c, land_w[1, 0, 1, OWN : OWN + rows])
+        ahead1 = jnp.where(lane == lanes - 1, roll(n1, lanes - 1), roll(m1, lanes - 1))
+        round2 = roll(m2, lanes - 2)
+        ahead2 = jnp.where(lane >= lanes - 2, roll(n2, lanes - 2), round2)
+        behind = roll(p1, 1)
+        lat_c[0, 0] = 1.0 - ahead1 + m0
+        lat_c[0, 1] = jnp.where(lane <= lanes - 2, ahead1 - ahead2, 0.0)
+        lat_c[0, 2] = jnp.where(lane <= lanes - 3, ahead2, 0.0)
+        lat_c[0, 3] = jnp.where(lane >= 1, behind - m0, 0.0)
+        lat_c[0, 4] = jnp.where(lane >= 2, -behind, 0.0)
+        last, first = jnp.logical_and(lane == lanes - 1, has_south), jnp.logical_and(lane == 0, has_north)
+        lat_c[1, 1] = jnp.where(last, roll(m1, lanes - 1) - round2, 0.0)
+        lat_c[1, 2] = jnp.where(jnp.logical_and(lane >= lanes - 2, has_south), round2, 0.0)
+        lat_c[1, 3] = jnp.where(first, behind - n0, 0.0)
+        second = jnp.logical_and(lane == 1, has_north)
+        lat_c[1, 4] = jnp.where(first, -behind, jnp.where(second, -roll(np1, 1), 0.0))
+
+    def push_lon():
+        down = lax.broadcasted_iota(jnp.int32, (tall_rows, lanes), 0)
+        across = lax.broadcasted_iota(jnp.int32, (tall_rows, lanes), 1)
+        faces = jnp.logical_and(down >= OWN, down <= OWN + rows)
+        here, south_of = cos_ref[my_lat], cos_ref[lax.rem(my_lat + nlat - 1, nlat)]
+        north_of = cos_ref[lax.rem(my_lat + 1, nlat)]
+        across1 = lax.broadcasted_iota(jnp.int32, (1, lanes), 1)
+        at_north = jnp.logical_and(across < 2, has_north)
+        at_south = jnp.logical_and(across >= lanes - 2, has_south)
+        sides = (
+            (ids[0], ids[1], here),
+            tuple(jnp.where(at_north, beside[1, m], jnp.where(at_south, beside[0, m], 0.0)) for m in range(2))
+            + (jnp.where(across1 < 2, north_of, south_of),),
+        )
+        for side, (courant, branch, cosine) in enumerate(sides):
+            m2, m1, m0, p1 = face_weights(jnp.where(faces, courant, 0.0), branch)
+            ahead1 = pltpu.roll(m1, tall_rows - 1, 0)
+            ahead2 = pltpu.roll(m2, tall_rows - 2, 0)
+            behind = pltpu.roll(p1, 1, 0)
+            found = (1.0 - ahead1 + m0, ahead1 - ahead2, ahead2, behind - m0, -behind)
+            for k, value in enumerate(found):
+                lon_c[side, k] = value[few] * cosine
+
+    def squeeze(value):
+        return jnp.sum(pltpu.roll(value, 0, 1, stride=4, stride_axis=0), axis=0, keepdims=True)
+
+    def halo_slots():
+        shape = (rows + 8, lanes)
+        down = lax.broadcasted_iota(jnp.int32, shape, 0)
+        across = lax.broadcasted_iota(jnp.int32, shape, 1)
+        at_north = jnp.logical_and(across < 2, has_north)
+        at_south = jnp.logical_and(across >= lanes - 2, has_south)
+        side = jnp.where(at_north, beside[1, 2, few], jnp.where(at_south, beside[0, 2, few], 0.0))
+        side = squeeze(jnp.where(down < rows + 4, side, 0.0)).astype(jnp.int32)
+        halo = [
+            (i, ids[2, OWN - 2 + i : OWN - 1 + i].astype(jnp.int32))
+            for i in (0, 1, rows + 2, rows + 3)
+        ]
+        find_slots(halo + [(rows + 4, side)])
+
+    def push_totals():
+        a = y_ref[0]
+        turned = (a, roll(a, lanes - 1), roll(a, lanes - 2), roll(a, 1), roll(a, 2))
+        for side in range(2):
+            value = lat_c[side, 1] * turned[1]
+            for k in range(2, 5):
+                value = value + lat_c[side, k] * turned[k]
+            if side == 0:
+                value = value + lat_c[0, 0] * a
+            bext[side, OWN : OWN + rows] = value
+        found = []
+        for side in range(2):
+            value = jnp.zeros((rows + 8, lanes), jnp.float32)
+            for k, step in enumerate((0, 1, 2, -1, -2)):
+                at = OWN - 2 + step
+                value = value + lon_c[side, k] * bext[side, at : at + rows + 8]
+            found.append(value)
+        regions(0, 0, [found[0][: rows + 4], squeeze(found[1])])
 
     get_mix[1].wait()
     coefficients(1)
@@ -376,16 +471,39 @@
     for copy in get_lon[1]:
         copy.wait()
     lon_own_weights(1)
+    for copy in get_lat[0]:
+        copy.wait()
+    pack_weights(0)
+    for copy in get_lon[0] + get_small:
+        copy.wait()
+    ids[0, OWN : OWN + rows] = lonc[0, 0]
+    ids[1, OWN : OWN + rows] = lonb[0, 0].astype(jnp.float32)
+    ids[2, OWN : OWN + rows] = rmap_ref[...].astype(jnp.float32)
+    bext[...] = jnp.zeros_like(bext)
     pl.semaphore_wait(barrier, count - 1)
 
     turn = {1: lax.rem(my_lon + 1, nlon), -1: lax.rem(my_lon + nlon - 1, nlon)}
     own_rows, first, last_two = pl.ds(OWN, rows), pl.ds(OWN, 2), pl.ds(OWN + rows - 2, 2)
     low, high = pl.ds(OWN - 2, 2), pl.ds(OWN + rows, 2)
 
+    class Guarded:
+        def __init__(self, copy, send_if, recv_if):
+            self.copy, self.send_if, self.recv_if = copy, send_if, recv_if
+
+        def start(self):
+            pl.when(self.send_if)(self.copy.start)
+
+        def wait_recv(self):
+            pl.when(self.recv_if)(self.copy.wait_recv)
+
+        def wait_send(self):
+            pl.when(self.send_if)(self.copy.wait_send)
+
     def send_columns(source, target, base):
         copies = []
         for end in range(2):
-            beside = (north, south)[end][1]
+            toward = (north, south)[end][1]
+            guards = ((has_north, has_south), (has_south, has_north))[end]
             for k, (lon, src, dst) in enumerate(
                 (
                     (my_lon, own_rows, own_rows),
@@ -393,9 +511,10 @@
                     (turn[-1], first, high),
                 )
             ):
-                copies.append(
-                    remote(source(end, src), target(end, dst), base + 3 * end + k, (lon, beside))
-                )
+                copy = remote(source(end, src), target(end, dst), base + 3 * end + k, (lon, toward), False)
+                copy = Guarded(copy, *guards)
+                copy.start()
+                copies.append(copy)
         return tuple(copies)
 
     def exchange(s, base):
@@ -418,42 +537,46 @@
     def group_of(device):
         return (device * width) // blk
 
-    def scatter(s):
-        def body(k, carry):
-            device = lax.rem(me + k, count)
-            pltpu.make_async_remote_copy(
-                src_ref=send_ref.at[s, group_of(device)],
-                dst_ref=land.at[s, me],
-                send_sem=all_sem.at[2 * s],
-                recv_sem=all_sem.at[2 * s + 1],
-                device_id=place(device),
-                device_id_type=MESH,
-            ).start()
-            return carry
-
-        lax.fori_loop(1, count, body, 0)
-        land[s, me] = send_ref[s, group_of(me)]
+    def scatter(k, carry):
+        device = lax.rem(me + k, count)
+        pltpu.make_async_remote_copy(
+            src_ref=send_ref.at[group_of(device)],
+            dst_ref=land.at[me],
+            send_sem=all_sem.at[0],
+            recv_sem=all_sem.at[1],
+            device_id=place(device),
+            device_id_type=MESH,
+        ).start()
+        return carry
+
+    def send_ids(base):
+        return (
+            remote(ids.at[:, last_two, :], ids.at[:, low, :], base, east),
+            remote(ids.at[:, first, :], ids.at[:, high, :], base + 1, west),
+        ) + send_columns(
+            lambda end, at: ids.at[:, at, :],
+            lambda end, at: beside.at[end, :, at, :],
+            base + 2,
+        )
 
     sent_a = {1: exchange(1, 0)}
     sent_w = {1: send_lat_weights(1, 16)}
+    sent_ids = send_ids(34)
     sent_lon = {1: send_lon(1, 28)}
+    sent_w[0] = send_lat_weights(0, 22)
     lat_inner(1)
     get_mix[0].wait()
     coefficients(0)
-    for copy in get_lat[0]:
-        copy.wait()
-    pack_weights(0)
-    sent_w[0] = send_lat_weights(0, 22)
-    for copy in get_lon[0]:
-        copy.wait()
     lon_own_weights(0)
     sent_lon[0] = send_lon(0, 31)
-    for copy in get_small:
-        copy.wait()
-    cosine = cos_ref[...]
-    find_slots()
-    for copy in sent_a[1] + sent_w[1]:
+    find_slots([(2 + i, rmap_ref[i : i + 1, :]) for i in range(rows)])
+    for copy in sent_w[0]:
         copy.wait_recv()
+    push_lat()
+    for copy in sent_ids + sent_a[1] + sent_w[1]:
+        copy.wait_recv()
+    push_lon()
+    halo_slots()
     lat_edges(1)
     for copy in sent_lon[1]:
         copy.wait_recv()
@@ -466,35 +589,35 @@
     solve(0)
     lat_rows(0)
     sent_a[0] = exchange(0, 8)
-    regions(1, x_ref[0] * cosine)
-    scatter(1)
+    push_totals()
+    regions(1, 2, [x_ref[0] * cos_ref[my_lat]])
+    lax.fori_loop(1, count, scatter, 0)
+    land[me] = send_ref[group_of(me)]
     lat_inner(0)
     get_cov.wait()
     covh[...] = covv[...].astype(jnp.bfloat16)
     covl[...] = (covv[...] - covh[...].astype(jnp.float32)).astype(jnp.bfloat16)
-    for copy in sent_a[0] + sent_w[0]:
+    for copy in sent_a[0]:
         copy.wait_recv()
     lat_edges(0)
     for copy in sent_lon[0]:
         copy.wait_recv()
-    start = lon_level(0, 0)
-    out_ref[0] = start
-    regions(0, start * cosine)
-    scatter(0)
 
     def last(level, carry):
         out_ref[level] = lon_level(0, level)
         return carry
 
-    lax.fori_loop(1, levels, last, 0, unroll=True)
+    lax.fori_loop(0, levels, last, 0, unroll=True)
+    put_out = fetch(out_ref, out_h, 15)
     for s in range(steps):
         for copy in sent_a[s] + sent_w[s] + sent_lon[s]:
             copy.wait_send()
-    for s in range(steps):
-        every = land.at[s, pl.ds(0, count - 1)]
-        pltpu.make_async_copy(every, every, all_sem.at[2 * s]).wait()
-        pltpu.make_async_copy(every, every, all_sem.at[2 * s + 1]).wait()
-    totals = jnp.concatenate([jnp.sum(land[s], axis=0) for s in range(steps)], axis=0)
+    for copy in sent_ids:
+        copy.wait_send()
+    every = land.at[pl.ds(0, count - 1)]
+    pltpu.make_async_copy(every, every, all_sem.at[0]).wait()
+    pltpu.make_async_copy(every, every, all_sem.at[1]).wait()
+    totals = jnp.sum(land[...], axis=0)
     coarse = totals.astype(jnp.bfloat16).astype(jnp.float32)
     both = jnp.concatenate([coarse, totals - coarse, jnp.zeros((8, lanes), jnp.float32)], axis=0)
     both = both.astype(jnp.bfloat16)
@@ -508,6 +631,20 @@
     one, two = product(slice(0, half)), product(slice(half, blk))
     for s in range(steps):
         flux_ref[s : s + 1, :] = one[2 * s : 2 * s + 1] + two[2 * s + 1 : 2 * s + 2]
+    put_flux = fetch(flux_ref, flux_h, 16)
+    put_out.wait()
+    put_flux.wait()
+
+
+def store(adjoint_v, flux_v, adjoint_h, flux_h, sem):
+    copies = (
+        pltpu.make_async_copy(adjoint_v, adjoint_h, sem.at[0]),
+        pltpu.make_async_copy(flux_v, flux_h, sem.at[1]),
+    )
+    for copy in copies:
+        copy.start()
+    for copy in copies:
+        copy.wait()
 
 
 def per_device(
@@ -537,9 +674,11 @@
     tall = (levels, rows + 2 * OWN, lanes)
     vm = pltpu.VMEM
     scratch = [
+        vm(field, f32),
+        vm((steps, blk), f32),
         vm((rows, lanes), i32),
         vm((regions // 128, 128), i32),
-        vm((1, lanes), f32),
+        vm((nlat, 1, lanes), f32),
         vm(field, f32),
         vm((steps, levels - 1, rows, lanes), f32),
         vm((steps,) + field, f32),
@@ -563,17 +702,20 @@
         vm((2, steps, 2 * levels + 8, lanes), f32),
         vm((2, steps, 2 * levels + 8, lanes), f32),
         vm((2, steps, 2, 2 * levels, lanes), f32),
-        vm((rows, lanes), f32),
-        vm((rows, lanes), f32),
-        vm((128, rows * lanes), b16),
-        vm((2 * (regions // 128), rows * lanes), b16),
-        vm((regions // 128, 128), f32),
-        vm((steps, regions // blk, 2, 128), f32),
-        vm((steps, nlon * nlat, 2, 128), f32),
-        pltpu.SemaphoreType.DMA((15,)),
-        pltpu.SemaphoreType.DMA((34,)),
-        pltpu.SemaphoreType.DMA((34,)),
-        pltpu.SemaphoreType.DMA((4,)),
+        vm((3, rows + 2 * OWN, lanes), f32),
+        vm((2, 3, rows + 2 * OWN, lanes), f32),
+        vm((2, 5, rows, lanes), f32),
+        vm((2, 5, rows + 8, lanes), f32),
+        vm((2, rows + 2 * OWN, lanes), f32),
+        vm((regions // 128, (rows + 5) * lanes), b16),
+        vm((128, (rows + 5) * lanes), b16),
+        vm((2 * (regions // 128), (rows + 5) * lanes), b16),
+        vm((regions // blk, 4, 128), f32),
+        vm((nlon * nlat, 4, 128), f32),
+        pltpu.SemaphoreType.DMA((17,)),
+        pltpu.SemaphoreType.DMA((42,)),
+        pltpu.SemaphoreType.DMA((42,)),
+        pltpu.SemaphoreType.DMA((2,)),
     ]
     adjoint, flux = pl.pallas_call(
         functools.partial(kernel, nlon, nlat, width),
@@ -583,8 +725,8 @@
         ),
         in_specs=[pl.BlockSpec(memory_space=pltpu.HBM)] * 10,
         out_specs=(
-            pl.BlockSpec(memory_space=pltpu.VMEM),
-            pl.BlockSpec(memory_space=pltpu.VMEM),
+            pl.BlockSpec(memory_space=pl.ANY),
+            pl.BlockSpec(memory_space=pl.ANY),
         ),
         scratch_shapes=scratch,
         compiler_params=pltpu.CompilerParams(
@@ -602,6 +744,16 @@
         region_order.reshape(regions // 128, 128),
         cosines,
     )
+    adjoint, flux = pl.pallas_call(
+        store,
+        out_shape=(
+            jax.ShapeDtypeStruct(field, f32),
+            jax.ShapeDtypeStruct((steps, blk), f32),
+        ),
+        in_specs=[pl.BlockSpec(memory_space=pl.ANY)] * 2,
+        out_specs=(pl.BlockSpec(memory_space=pl.ANY),) * 2,
+        scratch_shapes=[pltpu.SemaphoreType.DMA((2,))],
+    )(pltpu.with_memory_space_constraint(adjoint, pltpu.VMEM), pltpu.with_memory_space_constraint(flux, pltpu.VMEM))
     if width < blk:
         start = lax.rem(lax.axis_index("lat") * width, blk)
         flux = lax.dynamic_slice_in_dim(flux, start, width, 1)

time: 23.9 us -> 20.9 us (0.87)
  Pallas kernels: 21.8 us -> 20.1 us
  local copies, waits for them, and re-layouts: 1.29 us -> 0 us
    pallas_call x1, Pallas kernels: 21.8 us -> 19.4 us  [per_device(): pl.pallas_call(functools.partial(kernel, nlon, nlat, width), out_shape=(p...]
    unnamed x2 -> x0, local copies, waits for them, and re-layouts: 1.29 us -> none
    pallas_call x0 -> x1, Pallas kernels: none -> 0.73 us  [per_device(): pl.pallas_call(store, out_shape=(jax.ShapeDtypeStruct(field, f32), jax.Sh...]
where the time goes in v1:
time: 20.9 us; the launch traced here: 20.8 us
  Pallas kernels  20.1 us (96%)
  between operations  0.64 us (3%)
    pallas_call x1, Pallas kernels, per_device(): pl.pallas_call(functools.partial(kernel, nlon, nlat, width), out_shape=(p...  19.4 us
    pallas_call x1, Pallas kernels, per_device(): pl.pallas_call(store, out_shape=(jax.ShapeDtypeStruct(field, f32), jax.Sh...  0.73 us

profile of v1, /device:TPU:0, one launch (start us, length us, event | category | flops | bytes accessed | tf_op | source)
XLA Modules:
  0.0 20.8 jit_solution(2923008753232326589)
XLA Ops:
  0.6 19.4 %shard_map.113 = (f32[34,16,128]{2,1,0:T(8,128)S(1)}, f32[2,256]{1,0:T(2,128)S(1)}) custom-call(f32[34,16,128]{2,1,0:T(8,128)} %adj_h.1, f32[2,34,16,128]{3,2,1,0:T(8,128)} %lonc_h.1, s32[2,34,16,128]{3,2,1,0:T(8,128)} %lonb_h.1, f32[2,34,16,128]{3,2,1,0:T(8,128)} %latc_h.1, s32[2,34,16,128]{3,2,1,0:T(8,128)} %latb_h.1, f32[2,33,16,128]{3,2,1,0:T(8,128)} %mix_h.1, ...), custom_call_target="tpu_custom_call" | custom-call | tf_op jit(solution)/shard_map/pallas_call | solution.py:720
  20.0 0.7 %shard_map.114 = (f32[34,16,128]{2,1,0:T(8,128)}, f32[2,256]{1,0:T(2,128)}) custom-call(f32[34,16,128]{2,1,0:T(8,128)S(1)} %get-tuple-element.4.adjoint_v, f32[2,256]{1,0:T(2,128)S(1)} %get-tuple-element.5.flux_v), custom_call_target="tpu_custom_call" | custom-call | tf_op jit(solution)/shard_map/pallas_call | solution.py:747

commit v2 on v1

--- a/solution.py
+++ b/solution.py
@@ -63,10 +63,8 @@
     y_ref,
     ext,
     lw,
-    pack_w,
-    land_w,
-    pack_a,
-    land_a,
+    pack,
+    land_p,
     raw_rows,
     rows_a,
     far_a,
@@ -81,6 +79,7 @@
     amat,
     send_ref,
     land,
+    sizer,
     local_sem,
     send_sem,
     recv_sem,
@@ -98,31 +97,30 @@
     barrier = pltpu.get_barrier_semaphore()
 
     def fetch(src, dst, slot):
-        copy = pltpu.make_async_copy(src, dst, local_sem.at[slot])
-        copy.start()
-        return copy
-
-    get_mix, get_lat, get_lon = {}, {}, {}
-    get_mix[1] = fetch(mix_h.at[1], mixv.at[1], 0)
-    get_adj = fetch(adj_h, x_ref, 1)
-    for s in (1, 0):
-        at = 2 + 5 * (1 - s)
-        get_lat[s] = (
-            fetch(latc_h.at[s], latc.at[s], at),
-            fetch(latb_h.at[s], latb.at[s], at + 1),
-        )
-        get_lon[s] = (
-            fetch(lonc_h.at[s], lonc.at[s], at + 2),
-            fetch(lonb_h.at[s], lonb.at[s], at + 3),
-        )
-        if s == 1:
-            get_mix[0] = fetch(mix_h.at[0], mixv.at[0], at + 4)
-    get_small = (
-        fetch(rmap_h, rmap_ref, 11),
-        fetch(order_h, order_ref, 12),
-        fetch(cos_h, cos_ref, 13),
-    )
-    get_cov = fetch(cov_h.at[(my_lat * width) // blk], covv, 14)
+        pltpu.make_async_copy(src, dst, local_sem.at[slot]).start()
+
+    def drain(sem, count_rows):
+        part = sizer.at[pl.ds(0, count_rows)]
+        pltpu.make_async_copy(part, part, sem).wait()
+
+    def got(slot, count_rows):
+        drain(local_sem.at[slot], count_rows)
+
+    fetch(mix_h.at[1], mixv.at[1], 0)
+    fetch(adj_h, x_ref, 1)
+    fetch(latc_h.at[1], latc.at[1], 2)
+    fetch(latb_h.at[1], latb.at[1], 2)
+    fetch(lonc_h.at[1], lonc.at[1], 3)
+    fetch(lonb_h.at[1], lonb.at[1], 3)
+    fetch(latc_h.at[0], latc.at[0], 4)
+    fetch(latb_h.at[0], latb.at[0], 4)
+    fetch(lonc_h.at[0], lonc.at[0], 4)
+    fetch(lonb_h.at[0], lonb.at[0], 4)
+    fetch(rmap_h, rmap_ref, 5)
+    fetch(order_h, order_ref, 5)
+    fetch(cos_h, cos_ref, 5)
+    fetch(mix_h.at[0], mixv.at[0], 6)
+    fetch(cov_h.at[(my_lat * width) // blk], covv, 7)
 
     far_first = jnp.where(my_lon >= nlon // 2, 1, 0)
 
@@ -145,18 +143,15 @@
     def roll(value, shift):
         return pltpu.roll(value, shift, 1)
 
-    def remote(src, dst, slot, device, start=True):
-        copy = pltpu.make_async_remote_copy(
+    def remote(src, dst, send_slot, recv_slot, device):
+        pltpu.make_async_remote_copy(
             src_ref=src,
             dst_ref=dst,
-            send_sem=send_sem.at[slot],
-            recv_sem=recv_sem.at[slot],
+            send_sem=send_sem.at[send_slot],
+            recv_sem=recv_sem.at[recv_slot],
             device_id=device,
             device_id_type=MESH,
-        )
-        if start:
-            copy.start()
-        return copy
+        ).start()
 
     north = (my_lon, lax.rem(my_lat + 1, nlat))
     south = (my_lon, lax.rem(my_lat + nlat - 1, nlat))
@@ -210,7 +205,7 @@
         _, tail, head = lax.fori_loop(0, levels, down, (zero, zero, zero), unroll=True)
         head = roll(head, lanes - 2)
         for member, value in enumerate((tail, head)):
-            pack_a[s, member, OWN : OWN + rows] = value
+            pack[s, member, 0, OWN : OWN + rows] = value
             at = 2 * levels + 2 * member
             rows_a[0, s, at : at + 2] = value[rows - 2 :]
             rows_a[1, s, at : at + 2] = value[:2]
@@ -230,7 +225,7 @@
         found = ((ct, bt), (roll(ch, lanes - 2), roll(bh, lanes - 2)))
         for end in range(2):
             for member in range(2):
-                pack_w[end, s, member, OWN : OWN + rows] = found[end][member]
+                pack[s, end, 1 + member, OWN : OWN + rows] = found[end][member]
         for member in range(2):
             at = 2 * levels + 4 + 2 * member
             rows_a[0, s, at : at + 2] = found[1][member][rows - 2 :]
@@ -264,14 +259,14 @@
         even = lax.rem(lane, 2) == 0
         for side, where in enumerate((slice(OWN - 2, OWN), slice(OWN + rows, OWN + rows + 2))):
             for member in range(2):
-                pack_a[s, member, where] = far_a[side, s, at + 2 * member : at + 2 * member + 2]
+                pack[s, member, 0, where] = far_a[side, s, at + 2 * member : at + 2 * member + 2]
                 far = at + 4 + 2 * member
-                pack_w[1, s, member, where] = far_a[side, s, far : far + 2]
-        tail, head = pack_a[s, 0], pack_a[s, 1]
-        before, after = land_a[s, 0], land_a[s, 1]
-        m2_after, m1_after, _, _ = face_weights(land_w[1, s, 0], land_w[1, s, 1])
-        _, _, m0_head, p1_head = face_weights(pack_w[1, s, 0], pack_w[1, s, 1])
-        _, _, _, p1_before = face_weights(land_w[0, s, 0], land_w[0, s, 1])
+                pack[s, 1, 1 + member, where] = far_a[side, s, far : far + 2]
+        tail, head = pack[s, 0, 0], pack[s, 1, 0]
+        before, after = land_p[s, 0, 0], land_p[s, 1, 0]
+        m2_after, m1_after, _, _ = face_weights(land_p[s, 1, 1], land_p[s, 1, 2])
+        _, _, m0_head, p1_head = face_weights(pack[s, 1, 1], pack[s, 1, 2])
+        _, _, _, p1_before = face_weights(land_p[s, 0, 1], land_p[s, 0, 2])
         jump = after - jnp.where(even, roll(tail, lanes - 1), roll(after, 1))
         top = m2_after * jump + roll(jnp.where(even, m1_after * jump, 0.0), 1)
         top = jnp.where(my_lat < nlat - 1, top, 0.0)
@@ -316,23 +311,20 @@
         out = a[2] + w[0] * (a[4] - a[3]) + w[1] * (a[3] - a[2])
         return out + w[2] * (a[2] - a[1]) + w[3] * (a[1] - a[0])
 
-    def send_lon(s, base):
+    def send_lon(s):
         end = OWN + rows
-        return tuple(
+        for member, src, dst, size, device in (
+            (0, OWN, end, 2, west),
+            (1, OWN, end, 1, west),
+            (3, end - 1, OWN - 1, 1, east),
+        ):
             remote(
                 lw.at[s, member, :, pl.ds(src, size), :],
                 lw.at[s, member, :, pl.ds(dst, size), :],
-                base + k,
+                0,
+                s,
                 device,
             )
-            for k, (member, src, dst, size, device) in enumerate(
-                (
-                    (0, OWN, end, 2, west),
-                    (1, OWN, end, 1, west),
-                    (3, end - 1, OWN - 1, 1, east),
-                )
-            )
-        )
 
     def find_slots(found_rows):
         order = order_ref[...]
@@ -383,8 +375,8 @@
     def push_lat():
         courant = jnp.where(jnp.logical_and(lane == 0, my_lat == 0), 0.0, latc[0, 0])
         m2, m1, m0, p1 = face_weights(courant, latb[0, 0])
-        north_c = jnp.where(has_north, land_w[1, 0, 0, OWN : OWN + rows], 0.0)
-        n2, n1, n0, np1 = face_weights(north_c, land_w[1, 0, 1, OWN : OWN + rows])
+        north_c = jnp.where(has_north, land_p[0, 1, 1, OWN : OWN + rows], 0.0)
+        n2, n1, n0, np1 = face_weights(north_c, land_p[0, 1, 2, OWN : OWN + rows])
         ahead1 = jnp.where(lane == lanes - 1, roll(n1, lanes - 1), roll(m1, lanes - 1))
         round2 = roll(m2, lanes - 2)
         ahead2 = jnp.where(lane >= lanes - 2, roll(n2, lanes - 2), round2)
@@ -460,22 +452,18 @@
             found.append(value)
         regions(0, 0, [found[0][: rows + 4], squeeze(found[1])])
 
-    get_mix[1].wait()
+    got(0, (levels - 1) * rows)
     coefficients(1)
-    get_adj.wait()
+    got(1, levels * rows)
     solve(1)
-    for copy in get_lat[1]:
-        copy.wait()
+    got(2, 2 * levels * rows)
     pack_weights(1)
     lat_rows(1)
-    for copy in get_lon[1]:
-        copy.wait()
+    got(3, 2 * levels * rows)
     lon_own_weights(1)
-    for copy in get_lat[0]:
-        copy.wait()
+    got(4, 4 * levels * rows)
     pack_weights(0)
-    for copy in get_lon[0] + get_small:
-        copy.wait()
+    got(5, rows + order_ref.shape[0] + nlat)
     ids[0, OWN : OWN + rows] = lonc[0, 0]
     ids[1, OWN : OWN + rows] = lonb[0, 0].astype(jnp.float32)
     ids[2, OWN : OWN + rows] = rmap_ref[...].astype(jnp.float32)
@@ -486,53 +474,41 @@
     own_rows, first, last_two = pl.ds(OWN, rows), pl.ds(OWN, 2), pl.ds(OWN + rows - 2, 2)
     low, high = pl.ds(OWN - 2, 2), pl.ds(OWN + rows, 2)
 
-    class Guarded:
-        def __init__(self, copy, send_if, recv_if):
-            self.copy, self.send_if, self.recv_if = copy, send_if, recv_if
-
-        def start(self):
-            pl.when(self.send_if)(self.copy.start)
-
-        def wait_recv(self):
-            pl.when(self.recv_if)(self.copy.wait_recv)
-
-        def wait_send(self):
-            pl.when(self.send_if)(self.copy.wait_send)
-
-    def send_columns(source, target, base):
-        copies = []
+    toward = (north[1], south[1])
+    send_if, recv_if = (has_north, has_south), (has_south, has_north)
+    column_rows = rows + 4
+
+    def send_columns(source, target, recv_base):
         for end in range(2):
-            toward = (north, south)[end][1]
-            guards = ((has_north, has_south), (has_south, has_north))[end]
-            for k, (lon, src, dst) in enumerate(
-                (
-                    (my_lon, own_rows, own_rows),
+
+            @pl.when(send_if[end])
+            def _():
+                for lon, src, dst in (
                     (turn[1], last_two, low),
                     (turn[-1], first, high),
-                )
-            ):
-                copy = remote(source(end, src), target(end, dst), base + 3 * end + k, (lon, toward), False)
-                copy = Guarded(copy, *guards)
-                copy.start()
-                copies.append(copy)
-        return tuple(copies)
-
-    def exchange(s, base):
-        return (
-            remote(rows_a.at[0, s], far_a.at[0, s], base, east),
-            remote(rows_a.at[1, s], far_a.at[1, s], base + 1, west),
-        ) + send_columns(
-            lambda end, at: pack_a.at[s, end, at, :],
-            lambda end, at: land_a.at[s, end, at, :],
-            base + 2,
-        )
-
-    def send_lat_weights(s, base):
-        return send_columns(
-            lambda end, at: pack_w.at[end, s, :, at, :],
-            lambda end, at: land_w.at[end, s, :, at, :],
-            base,
-        )
+                    (my_lon, own_rows, own_rows),
+                ):
+                    remote(
+                        source(end, src),
+                        target(end, dst),
+                        1 + end,
+                        recv_base + end,
+                        (lon, toward[end]),
+                    )
+
+    def got_columns(recv_base, members):
+        for end in range(2):
+
+            @pl.when(recv_if[end])
+            def _():
+                drain(recv_sem.at[recv_base + end], members * column_rows)
+
+    def send_border(s):
+        remote(rows_a.at[0, s], far_a.at[0, s], 0, 2 + s, east)
+        remote(rows_a.at[1, s], far_a.at[1, s], 0, 2 + s, west)
+
+    border_rows = 2 * rows_a.shape[2]
+    lon_rows = 4 * levels
 
     def group_of(device):
         return (device * width) // blk
@@ -549,71 +525,72 @@
         ).start()
         return carry
 
-    def send_ids(base):
-        return (
-            remote(ids.at[:, last_two, :], ids.at[:, low, :], base, east),
-            remote(ids.at[:, first, :], ids.at[:, high, :], base + 1, west),
-        ) + send_columns(
-            lambda end, at: ids.at[:, at, :],
-            lambda end, at: beside.at[end, :, at, :],
-            base + 2,
-        )
-
-    sent_a = {1: exchange(1, 0)}
-    sent_w = {1: send_lat_weights(1, 16)}
-    sent_ids = send_ids(34)
-    sent_lon = {1: send_lon(1, 28)}
-    sent_w[0] = send_lat_weights(0, 22)
+    send_columns(
+        lambda end, at: pack.at[1, end, :, at, :], lambda end, at: land_p.at[1, end, :, at, :], 5
+    )
+    remote(ids.at[:, last_two, :], ids.at[:, low, :], 0, 4, east)
+    remote(ids.at[:, first, :], ids.at[:, high, :], 0, 4, west)
+    send_columns(lambda end, at: ids.at[:, at, :], lambda end, at: beside.at[end, :, at, :], 7)
+    send_columns(
+        lambda end, at: pack.at[0, end, 1:3, at, :],
+        lambda end, at: land_p.at[0, end, 1:3, at, :],
+        7,
+    )
+    send_border(1)
+    send_lon(1)
     lat_inner(1)
-    get_mix[0].wait()
+    got(6, (levels - 1) * rows)
     coefficients(0)
     lon_own_weights(0)
-    sent_lon[0] = send_lon(0, 31)
+    send_lon(0)
     find_slots([(2 + i, rmap_ref[i : i + 1, :]) for i in range(rows)])
-    for copy in sent_w[0]:
-        copy.wait_recv()
+    drain(recv_sem.at[4], 12)
+    got_columns(7, 5)
     push_lat()
-    for copy in sent_ids + sent_a[1] + sent_w[1]:
-        copy.wait_recv()
     push_lon()
     halo_slots()
+    got_columns(5, 3)
+    drain(recv_sem.at[3], border_rows)
+    drain(recv_sem.at[1], lon_rows)
     lat_edges(1)
-    for copy in sent_lon[1]:
-        copy.wait_recv()
 
     def middle(level, carry):
         x_ref[level] = lon_level(1, level)
         return carry
 
     lax.fori_loop(0, levels, middle, 0, unroll=True)
+    regions(1, 2, [x_ref[0] * cos_ref[my_lat]])
     solve(0)
     lat_rows(0)
-    sent_a[0] = exchange(0, 8)
+    send_columns(
+        lambda end, at: pack.at[0, end, 0, at, :], lambda end, at: land_p.at[0, end, 0, at, :], 9
+    )
+    send_border(0)
     push_totals()
-    regions(1, 2, [x_ref[0] * cos_ref[my_lat]])
     lax.fori_loop(1, count, scatter, 0)
     land[me] = send_ref[group_of(me)]
     lat_inner(0)
-    get_cov.wait()
+    got(7, blk * blk // lanes)
     covh[...] = covv[...].astype(jnp.bfloat16)
     covl[...] = (covv[...] - covh[...].astype(jnp.float32)).astype(jnp.bfloat16)
-    for copy in sent_a[0]:
-        copy.wait_recv()
+    got_columns(9, 1)
+    drain(recv_sem.at[2], border_rows)
+    drain(recv_sem.at[0], lon_rows)
     lat_edges(0)
-    for copy in sent_lon[0]:
-        copy.wait_recv()
 
     def last(level, carry):
         out_ref[level] = lon_level(0, level)
         return carry
 
     lax.fori_loop(0, levels, last, 0, unroll=True)
-    put_out = fetch(out_ref, out_h, 15)
-    for s in range(steps):
-        for copy in sent_a[s] + sent_w[s] + sent_lon[s]:
-            copy.wait_send()
-    for copy in sent_ids:
-        copy.wait_send()
+    fetch(out_ref, out_h, 8)
+    drain(send_sem.at[0], 2 * (border_rows + lon_rows) + 12)
+    for end in range(2):
+
+        @pl.when(send_if[end])
+        def _():
+            drain(send_sem.at[1 + end], 9 * column_rows)
+
     every = land.at[pl.ds(0, count - 1)]
     pltpu.make_async_copy(every, every, all_sem.at[0]).wait()
     pltpu.make_async_copy(every, every, all_sem.at[1]).wait()
@@ -631,9 +608,8 @@
     one, two = product(slice(0, half)), product(slice(half, blk))
     for s in range(steps):
         flux_ref[s : s + 1, :] = one[2 * s : 2 * s + 1] + two[2 * s + 1 : 2 * s + 2]
-    put_flux = fetch(flux_ref, flux_h, 16)
-    put_out.wait()
-    put_flux.wait()
+    fetch(flux_ref, flux_h, 8)
+    got(8, levels * rows + steps * blk // lanes)
 
 
 def store(adjoint_v, flux_v, adjoint_h, flux_h, sem):
@@ -694,10 +670,8 @@
         vm(field, f32),
         vm((steps,) + tall, f32),
         vm((steps, 4) + tall, f32),
-        vm((2, steps, 2, rows + 2 * OWN, lanes), f32),
-        vm((2, steps, 2, rows + 2 * OWN, lanes), f32),
-        vm((steps, 2, rows + 2 * OWN, lanes), f32),
-        vm((steps, 2, rows + 2 * OWN, lanes), f32),
+        vm((steps, 2, 3, rows + 2 * OWN, lanes), f32),
+        vm((steps, 2, 3, rows + 2 * OWN, lanes), f32),
         vm((2, 2 * levels, lanes), f32),
         vm((2, steps, 2 * levels + 8, lanes), f32),
         vm((2, steps, 2 * levels + 8, lanes), f32),
@@ -712,9 +686,10 @@
         vm((2 * (regions // 128), (rows + 5) * lanes), b16),
         vm((regions // blk, 4, 128), f32),
         vm((nlon * nlat, 4, 128), f32),
-        pltpu.SemaphoreType.DMA((17,)),
-        pltpu.SemaphoreType.DMA((42,)),
-        pltpu.SemaphoreType.DMA((42,)),
+        vm((4 * levels * rows, lanes), f32),
+        pltpu.SemaphoreType.DMA((9,)),
+        pltpu.SemaphoreType.DMA((3,)),
+        pltpu.SemaphoreType.DMA((11,)),
         pltpu.SemaphoreType.DMA((2,)),
     ]
     adjoint, flux = pl.pallas_call(

time: 20.9 us -> 19.3 us (0.923)
  Pallas kernels: 20.1 us -> 18.5 us
    pallas_call x1, Pallas kernels: 19.4 us -> 17.8 us  [per_device(): pl.pallas_call(functools.partial(kernel, nlon, nlat, width), out_shape=(p...]
where the time goes in v2:
time: 19.3 us; the launch traced here: 19.1 us
  Pallas kernels  18.5 us (96%)
  between operations  0.64 us (3%)
    pallas_call x1, Pallas kernels, per_device(): pl.pallas_call(functools.partial(kernel, nlon, nlat, width), out_shape=(p...  17.8 us
    pallas_call x1, Pallas kernels, per_device(): pl.pallas_call(store, out_shape=(jax.ShapeDtypeStruct(field, f32), jax.Sh...  0.73 us

profile of v2, /device:TPU:0, one launch (start us, length us, event | category | flops | bytes accessed | tf_op | source)
XLA Modules:
  0.0 19.1 jit_solution(8591099673212157775)
XLA Ops:
  0.6 17.8 %shard_map.113 = (f32[34,16,128]{2,1,0:T(8,128)S(1)}, f32[2,256]{1,0:T(2,128)S(1)}) custom-call(f32[34,16,128]{2,1,0:T(8,128)} %adj_h.1, f32[2,34,16,128]{3,2,1,0:T(8,128)} %lonc_h.1, s32[2,34,16,128]{3,2,1,0:T(8,128)} %lonb_h.1, f32[2,34,16,128]{3,2,1,0:T(8,128)} %latc_h.1, s32[2,34,16,128]{3,2,1,0:T(8,128)} %latb_h.1, f32[2,33,16,128]{3,2,1,0:T(8,128)} %mix_h.1, ...), custom_call_target="tpu_custom_call" | custom-call | tf_op jit(solution)/shard_map/pallas_call | solution.py:695
  18.4 0.7 %shard_map.114 = (f32[34,16,128]{2,1,0:T(8,128)}, f32[2,256]{1,0:T(2,128)}) custom-call(f32[34,16,128]{2,1,0:T(8,128)S(1)} %get-tuple-element.4.adjoint_v, f32[2,256]{1,0:T(2,128)S(1)} %get-tuple-element.5.flux_v), custom_call_target="tpu_custom_call" | custom-call | tf_op jit(solution)/shard_map/pallas_call | solution.py:722

commit v3 on v2

--- a/solution.py
+++ b/solution.py
@@ -106,6 +106,18 @@
     def got(slot, count_rows):
         drain(local_sem.at[slot], count_rows)
 
+    far_first = jnp.where(my_lon >= nlon // 2, 1, 0)
+
+    def greet(k, carry):
+        device = far_first * k + (1 - far_first) * (count - 1 - k)
+
+        @pl.when(device != me)
+        def _():
+            pl.semaphore_signal(barrier, inc=1, device_id=place(device), device_id_type=MESH)
+
+        return carry
+
+    lax.fori_loop(0, count // 4, greet, 0)
     fetch(mix_h.at[1], mixv.at[1], 0)
     fetch(adj_h, x_ref, 1)
     fetch(latc_h.at[1], latc.at[1], 2)
@@ -121,19 +133,7 @@
     fetch(cos_h, cos_ref, 5)
     fetch(mix_h.at[0], mixv.at[0], 6)
     fetch(cov_h.at[(my_lat * width) // blk], covv, 7)
-
-    far_first = jnp.where(my_lon >= nlon // 2, 1, 0)
-
-    def greet(k, carry):
-        device = far_first * k + (1 - far_first) * (count - 1 - k)
-
-        @pl.when(device != me)
-        def _():
-            pl.semaphore_signal(barrier, inc=1, device_id=place(device), device_id_type=MESH)
-
-        return carry
-
-    lax.fori_loop(0, count, greet, 0)
+    lax.fori_loop(count // 4, count, greet, 0)
 
     lane = lax.broadcasted_iota(jnp.int32, (rows, lanes), 1)
     pair = lane // 2
@@ -206,7 +206,7 @@
         head = roll(head, lanes - 2)
         for member, value in enumerate((tail, head)):
             pack[s, member, 0, OWN : OWN + rows] = value
-            at = 2 * levels + 2 * member
+            at = 2 * member
             rows_a[0, s, at : at + 2] = value[rows - 2 :]
             rows_a[1, s, at : at + 2] = value[:2]
 
@@ -227,13 +227,13 @@
             for member in range(2):
                 pack[s, end, 1 + member, OWN : OWN + rows] = found[end][member]
         for member in range(2):
-            at = 2 * levels + 4 + 2 * member
+            at = 4 + 2 * member
             rows_a[0, s, at : at + 2] = found[1][member][rows - 2 :]
             rows_a[1, s, at : at + 2] = found[1][member][:2]
 
     def lat_rows(s):
         for side in range(2):
-            rows_a[side, s, : 2 * levels] = lat_pass(
+            rows_a[side, s, 8:] = lat_pass(
                 raw_rows[side], rows_w[side, s, 0], rows_w[side, s, 1]
             )
 
@@ -253,20 +253,15 @@
 
         lax.fori_loop(0, levels, body, 0, unroll=True)
 
-    def lat_edges(s):
-        at = 2 * levels
-        lane = lax.broadcasted_iota(jnp.int32, (rows + 2 * OWN, lanes), 1)
+    def edge_terms(s, at):
+        count_rows = at.stop - at.start
+        lane = lax.broadcasted_iota(jnp.int32, (count_rows, lanes), 1)
         even = lax.rem(lane, 2) == 0
-        for side, where in enumerate((slice(OWN - 2, OWN), slice(OWN + rows, OWN + rows + 2))):
-            for member in range(2):
-                pack[s, member, 0, where] = far_a[side, s, at + 2 * member : at + 2 * member + 2]
-                far = at + 4 + 2 * member
-                pack[s, 1, 1 + member, where] = far_a[side, s, far : far + 2]
-        tail, head = pack[s, 0, 0], pack[s, 1, 0]
-        before, after = land_p[s, 0, 0], land_p[s, 1, 0]
-        m2_after, m1_after, _, _ = face_weights(land_p[s, 1, 1], land_p[s, 1, 2])
-        _, _, m0_head, p1_head = face_weights(pack[s, 1, 1], pack[s, 1, 2])
-        _, _, _, p1_before = face_weights(land_p[s, 0, 1], land_p[s, 0, 2])
+        tail, head = pack[s, 0, 0, at], pack[s, 1, 0, at]
+        before, after = land_p[s, 0, 0, at], land_p[s, 1, 0, at]
+        m2_after, m1_after, _, _ = face_weights(land_p[s, 1, 1, at], land_p[s, 1, 2, at])
+        _, _, m0_head, p1_head = face_weights(pack[s, 1, 1, at], pack[s, 1, 2, at])
+        _, _, _, p1_before = face_weights(land_p[s, 0, 1, at], land_p[s, 0, 2, at])
         jump = after - jnp.where(even, roll(tail, lanes - 1), roll(after, 1))
         top = m2_after * jump + roll(jnp.where(even, m1_after * jump, 0.0), 1)
         top = jnp.where(my_lat < nlat - 1, top, 0.0)
@@ -278,18 +273,32 @@
         both = (jnp.where(first, top, low), jnp.where(first, low, top))
         edge = jnp.logical_or(lane < 2, lane >= lanes - 2)
 
-        def body(m, carry):
-            for odd in range(2):
-                level = 2 * m + odd
-                turned = jnp.where(edge, roll(both[odd], lanes - 2 - 2 * level), 0.0)
-                ext[s, level, OWN : OWN + rows] += turned[OWN : OWN + rows]
-                two = pl.ds(2 * level, 2)
-                end = OWN + rows
-                ext[s, level, OWN - 2 : OWN] = far_a[0, s, two, :] + turned[OWN - 2 : OWN]
-                ext[s, level, end : end + 2] = far_a[1, s, two, :] + turned[end : end + 2]
-            return carry
-
-        lax.fori_loop(0, levels // 2, body, 0, unroll=True)
+        def at_level(level):
+            return jnp.where(edge, roll(both[level % 2], lanes - 2 - 2 * level), 0.0)
+
+        return at_level
+
+    def own_edges(s):
+        terms = edge_terms(s, slice(OWN, OWN + rows))
+        for level in range(levels):
+            ext[s, level, OWN : OWN + rows] += terms(level)
+
+    def far_terms(s):
+        for side, where in enumerate((slice(OWN - 2, OWN), slice(OWN + rows, OWN + rows + 2))):
+            for member in range(2):
+                pack[s, member, 0, where] = far_a[side, s, 2 * member : 2 * member + 2]
+                far = 4 + 2 * member
+                pack[s, 1, 1 + member, where] = far_a[side, s, far : far + 2]
+        return edge_terms(s, slice(0, OWN)), edge_terms(s, slice(OWN + rows, 2 * OWN + rows))
+
+    def edges_and_lon(s, target, terms, part):
+        end = OWN + rows
+        for level in range(*part):
+            two = slice(8 + 2 * level, 10 + 2 * level)
+            ext[s, level, OWN - 2 : OWN] = far_a[0, s, two] + terms[0](level)[OWN - 2 :]
+            ext[s, level, end : end + 2] = far_a[1, s, two] + terms[1](level)[:2]
+        for level in range(*part):
+            target[level] = lon_level(s, level)
 
     def lon_own_weights(s):
         def body(level, carry):
@@ -311,62 +320,69 @@
         out = a[2] + w[0] * (a[4] - a[3]) + w[1] * (a[3] - a[2])
         return out + w[2] * (a[2] - a[1]) + w[3] * (a[1] - a[0])
 
-    def send_lon(s):
+    def send_lon(s, part, slot):
         end = OWN + rows
         for member, src, dst, size, device in (
             (0, OWN, end, 2, west),
             (1, OWN, end, 1, west),
             (3, end - 1, OWN - 1, 1, east),
         ):
+            at = pl.ds(part[0], part[1] - part[0])
             remote(
-                lw.at[s, member, :, pl.ds(src, size), :],
-                lw.at[s, member, :, pl.ds(dst, size), :],
+                lw.at[s, member, at, pl.ds(src, size), :],
+                lw.at[s, member, at, pl.ds(dst, size), :],
                 0,
-                s,
+                slot,
                 device,
             )
 
-    def find_slots(found_rows):
+    def find_slots():
         order = order_ref[...]
-        table = jnp.concatenate([order // 128, lax.rem(order, 128)], axis=0)
+        table = jnp.concatenate([order // blk, lax.rem(order, blk)], axis=0)
         table = table.astype(jnp.float32).astype(jnp.bfloat16)
         high = order.shape[0]
         down = lax.broadcasted_iota(jnp.int32, (lanes, lanes), 0)
         row_of = lax.broadcasted_iota(jnp.int32, (high, lanes), 0)
-        for i, region in found_rows:
+        for i in range(rows):
+            region = rmap_ref[i : i + 1, :]
             hit = jnp.where(down == lax.rem(region, 128), 1.0, 0.0).astype(jnp.bfloat16)
             found = jnp.dot(table, hit, preferred_element_type=jnp.float32)
-            here = row_of == region // 128
-            hi = jnp.sum(jnp.where(here, found[:high], 0.0), axis=0, keepdims=True)
-            lo = jnp.sum(jnp.where(here, found[high:], 0.0), axis=0, keepdims=True)
-            at = slice(i * lanes, (i + 1) * lanes)
-            hot[:, at] = jnp.where(row_of.astype(jnp.float32) == hi, 1.0, 0.0).astype(jnp.bfloat16)
-            cht[:, at] = jnp.where(down.astype(jnp.float32) == lo, 1.0, 0.0).astype(jnp.bfloat16)
-
-    def regions(s, first, fields):
-        high = order_ref.shape[0]
-        coarse = [field.astype(jnp.bfloat16).astype(jnp.float32) for field in fields]
-        fine = [field - part for field, part in zip(fields, coarse)]
-        at = first
-        for field in range(len(fields)):
-            for i in range(fields[field].shape[0]):
-                here = slice(at * lanes, (at + 1) * lanes)
-                for part, values in enumerate((coarse, fine)):
-                    value = jnp.broadcast_to(values[field][i : i + 1], (high, lanes))
-                    amat[part * high : (part + 1) * high, here] = hot[:, here] * value.astype(
-                        jnp.bfloat16
+            both = found[:high] * float(blk) + found[high:]
+            both = jnp.where(row_of == region // 128, both, 0.0)
+            ids[2, OWN + i : OWN + i + 1] = jnp.sum(both, axis=0, keepdims=True)
+
+    def spread(i, slot):
+        groups = hot.shape[0] // 2
+        slot = slot.astype(jnp.int32)
+        high = lax.broadcasted_iota(jnp.int32, (2 * groups, lanes), 0) // 2
+        low = lax.broadcasted_iota(jnp.int32, (blk, lanes), 0)
+        at = slice(i * lanes, (i + 1) * lanes)
+        hot[:, at] = jnp.where(high == slot // blk, 1.0, 0.0).astype(jnp.bfloat16)
+        cht[:, at] = jnp.where(low == lax.rem(slot, blk), 1.0, 0.0).astype(jnp.bfloat16)
+
+    def regions(pushed, side, later):
+        tile, many = 16, hot.shape[0]
+        step0 = lax.rem(lax.broadcasted_iota(jnp.int32, (tile, lanes), 0), 2) == 0
+        for i in range(rows + 5):
+            here = slice(i * lanes, (i + 1) * lanes)
+            first = pushed[i : i + 1] if i < rows + 4 else side
+            second = later[i - 2 : i - 1] if 2 <= i < rows + 2 else jnp.zeros_like(first)
+            value = jnp.where(
+                step0, jnp.broadcast_to(first, (tile, lanes)), jnp.broadcast_to(second, (tile, lanes))
+            )
+            coarse = value.astype(jnp.bfloat16)
+            fine = (value - coarse.astype(jnp.float32)).astype(jnp.bfloat16)
+            for part, piece in enumerate((coarse, fine)):
+                for at in range(0, many, tile):
+                    amat[part * many + at : part * many + at + tile, here] = (
+                        hot[at : at + tile, here] * piece
                     )
-                at += 1
-        every = slice(first * lanes, at * lanes)
         sums = lax.dot_general(
-            amat[:, every],
-            cht[:, every],
-            (((1,), (1,)), ((), ())),
-            preferred_element_type=jnp.float32,
+            amat[...], cht[...], (((1,), (1,)), ((), ())), preferred_element_type=jnp.float32
         )
-        sums = sums[:high] + sums[high:]
-        for group in range(high // 2):
-            send_ref[group, 2 * s : 2 * s + 2, :] = sums[2 * group : 2 * group + 2]
+        sums = sums[:many] + sums[many:]
+        for group in range(many // 2):
+            send_ref[group] = sums[2 * group : 2 * group + 2]
 
     tall_rows = rows + 2 * OWN
     few = slice(OWN - 2, OWN + rows + 6)
@@ -375,8 +391,8 @@
     def push_lat():
         courant = jnp.where(jnp.logical_and(lane == 0, my_lat == 0), 0.0, latc[0, 0])
         m2, m1, m0, p1 = face_weights(courant, latb[0, 0])
-        north_c = jnp.where(has_north, land_p[0, 1, 1, OWN : OWN + rows], 0.0)
-        n2, n1, n0, np1 = face_weights(north_c, land_p[0, 1, 2, OWN : OWN + rows])
+        north_c = jnp.where(has_north, beside[1, 3, OWN : OWN + rows], 0.0)
+        n2, n1, n0, np1 = face_weights(north_c, beside[1, 4, OWN : OWN + rows])
         ahead1 = jnp.where(lane == lanes - 1, roll(n1, lanes - 1), roll(m1, lanes - 1))
         round2 = roll(m2, lanes - 2)
         ahead2 = jnp.where(lane >= lanes - 2, roll(n2, lanes - 2), round2)
@@ -393,7 +409,7 @@
         second = jnp.logical_and(lane == 1, has_north)
         lat_c[1, 4] = jnp.where(first, -behind, jnp.where(second, -roll(np1, 1), 0.0))
 
-    def push_lon():
+    def push_lon(side):
         down = lax.broadcasted_iota(jnp.int32, (tall_rows, lanes), 0)
         across = lax.broadcasted_iota(jnp.int32, (tall_rows, lanes), 1)
         faces = jnp.logical_and(down >= OWN, down <= OWN + rows)
@@ -402,36 +418,34 @@
         across1 = lax.broadcasted_iota(jnp.int32, (1, lanes), 1)
         at_north = jnp.logical_and(across < 2, has_north)
         at_south = jnp.logical_and(across >= lanes - 2, has_south)
-        sides = (
-            (ids[0], ids[1], here),
-            tuple(jnp.where(at_north, beside[1, m], jnp.where(at_south, beside[0, m], 0.0)) for m in range(2))
-            + (jnp.where(across1 < 2, north_of, south_of),),
-        )
-        for side, (courant, branch, cosine) in enumerate(sides):
-            m2, m1, m0, p1 = face_weights(jnp.where(faces, courant, 0.0), branch)
-            ahead1 = pltpu.roll(m1, tall_rows - 1, 0)
-            ahead2 = pltpu.roll(m2, tall_rows - 2, 0)
-            behind = pltpu.roll(p1, 1, 0)
-            found = (1.0 - ahead1 + m0, ahead1 - ahead2, ahead2, behind - m0, -behind)
-            for k, value in enumerate(found):
-                lon_c[side, k] = value[few] * cosine
+        if side == 0:
+            courant, branch, cosine = ids[0], ids[1], here
+        else:
+            courant, branch = (
+                jnp.where(at_north, beside[1, m], jnp.where(at_south, beside[0, m], 0.0))
+                for m in range(2)
+            )
+            cosine = jnp.where(across1 < 2, north_of, south_of)
+        m2, m1, m0, p1 = face_weights(jnp.where(faces, courant, 0.0), branch)
+        ahead1 = pltpu.roll(m1, tall_rows - 1, 0)
+        ahead2 = pltpu.roll(m2, tall_rows - 2, 0)
+        behind = pltpu.roll(p1, 1, 0)
+        found = (1.0 - ahead1 + m0, ahead1 - ahead2, ahead2, behind - m0, -behind)
+        for k, value in enumerate(found):
+            lon_c[side, k] = value[few] * cosine
 
     def squeeze(value):
         return jnp.sum(pltpu.roll(value, 0, 1, stride=4, stride_axis=0), axis=0, keepdims=True)
 
-    def halo_slots():
+    def side_slots():
         shape = (rows + 8, lanes)
         down = lax.broadcasted_iota(jnp.int32, shape, 0)
         across = lax.broadcasted_iota(jnp.int32, shape, 1)
         at_north = jnp.logical_and(across < 2, has_north)
         at_south = jnp.logical_and(across >= lanes - 2, has_south)
         side = jnp.where(at_north, beside[1, 2, few], jnp.where(at_south, beside[0, 2, few], 0.0))
-        side = squeeze(jnp.where(down < rows + 4, side, 0.0)).astype(jnp.int32)
-        halo = [
-            (i, ids[2, OWN - 2 + i : OWN - 1 + i].astype(jnp.int32))
-            for i in (0, 1, rows + 2, rows + 3)
-        ]
-        find_slots(halo + [(rows + 4, side)])
+        side = squeeze(jnp.where(down < rows + 4, side, 0.0))
+        spread(rows + 4, side)
 
     def push_totals():
         a = y_ref[0]
@@ -450,7 +464,7 @@
                 at = OWN - 2 + step
                 value = value + lon_c[side, k] * bext[side, at : at + rows + 8]
             found.append(value)
-        regions(0, 0, [found[0][: rows + 4], squeeze(found[1])])
+        regions(found[0], squeeze(found[1]), x_ref[0] * cos_ref[my_lat])
 
     got(0, (levels - 1) * rows)
     coefficients(1)
@@ -462,11 +476,12 @@
     got(3, 2 * levels * rows)
     lon_own_weights(1)
     got(4, 4 * levels * rows)
-    pack_weights(0)
     got(5, rows + order_ref.shape[0] + nlat)
     ids[0, OWN : OWN + rows] = lonc[0, 0]
     ids[1, OWN : OWN + rows] = lonb[0, 0].astype(jnp.float32)
-    ids[2, OWN : OWN + rows] = rmap_ref[...].astype(jnp.float32)
+    ids[3, OWN : OWN + rows] = latc[0, 0]
+    ids[4, OWN : OWN + rows] = latb[0, 0].astype(jnp.float32)
+    find_slots()
     bext[...] = jnp.zeros_like(bext)
     pl.semaphore_wait(barrier, count - 1)
 
@@ -478,36 +493,44 @@
     send_if, recv_if = (has_north, has_south), (has_south, has_north)
     column_rows = rows + 4
 
-    def send_columns(source, target, recv_base):
+    def send_columns(source, target, recv_base, diagonal):
         for end in range(2):
 
             @pl.when(send_if[end])
             def _():
                 for lon, src, dst in (
-                    (turn[1], last_two, low),
-                    (turn[-1], first, high),
-                    (my_lon, own_rows, own_rows),
+                    ((turn[1], last_two, low), (turn[-1], first, high))
+                    if diagonal
+                    else ((my_lon, own_rows, own_rows),)
                 ):
                     remote(
                         source(end, src),
                         target(end, dst),
-                        1 + end,
-                        recv_base + end,
+                        1,
+                        recv_base + (1 if diagonal else 0),
                         (lon, toward[end]),
                     )
 
-    def got_columns(recv_base, members):
-        for end in range(2):
-
-            @pl.when(recv_if[end])
+    beside_count = jnp.where(has_north, 1, 0) + jnp.where(has_south, 1, 0)
+
+    def drain_beside(sem, count_rows):
+        for ends in (1, 2):
+
+            @pl.when(beside_count == ends)
             def _():
-                drain(recv_sem.at[recv_base + end], members * column_rows)
-
-    def send_border(s):
-        remote(rows_a.at[0, s], far_a.at[0, s], 0, 2 + s, east)
-        remote(rows_a.at[1, s], far_a.at[1, s], 0, 2 + s, west)
-
-    border_rows = 2 * rows_a.shape[2]
+                drain(sem, ends * count_rows)
+
+    half = levels // 2
+    parts = ((0, half), (half, levels))
+    spans = (pl.ds(0, 8 + 2 * half), pl.ds(8 + 2 * half, 2 * (levels - half)))
+    border = (2 * (8 + 2 * half), 4 * (levels - half))
+
+    def send_border(s, part, slot):
+        at = spans[part]
+        remote(rows_a.at[0, s, at, :], far_a.at[0, s, at, :], 0, slot, east)
+        remote(rows_a.at[1, s, at, :], far_a.at[1, s, at, :], 0, slot, west)
+
+    border_rows = sum(border)
     lon_rows = 4 * levels
 
     def group_of(device):
@@ -525,47 +548,78 @@
         ).start()
         return carry
 
-    send_columns(
-        lambda end, at: pack.at[1, end, :, at, :], lambda end, at: land_p.at[1, end, :, at, :], 5
-    )
-    remote(ids.at[:, last_two, :], ids.at[:, low, :], 0, 4, east)
-    remote(ids.at[:, first, :], ids.at[:, high, :], 0, 4, west)
-    send_columns(lambda end, at: ids.at[:, at, :], lambda end, at: beside.at[end, :, at, :], 7)
-    send_columns(
-        lambda end, at: pack.at[0, end, 1:3, at, :],
-        lambda end, at: land_p.at[0, end, 1:3, at, :],
-        7,
-    )
-    send_border(1)
-    send_lon(1)
+    three = pl.ds(0, 3)
+
+    def send_packs(diagonal):
+        send_columns(
+            lambda end, at: pack.at[1, end, :, at, :],
+            lambda end, at: land_p.at[1, end, :, at, :],
+            5,
+            diagonal,
+        )
+        if diagonal:
+            send_columns(
+                lambda end, at: ids.at[three, at, :],
+                lambda end, at: beside.at[end, three, at, :],
+                7,
+                True,
+            )
+        else:
+            send_columns(
+                lambda end, at: ids.at[:, at, :], lambda end, at: beside.at[end, :, at, :], 7, False
+            )
+
+    send_packs(True)
+    remote(ids.at[three, last_two, :], ids.at[three, low, :], 0, 4, east)
+    remote(ids.at[three, first, :], ids.at[three, high, :], 0, 4, west)
+    for part, slot in ((0, 1), (1, 3)):
+        send_border(1, part, slot)
+        if part == 0:
+            send_packs(False)
+        send_lon(1, parts[part], slot)
     lat_inner(1)
     got(6, (levels - 1) * rows)
     coefficients(0)
     lon_own_weights(0)
-    send_lon(0)
-    find_slots([(2 + i, rmap_ref[i : i + 1, :]) for i in range(rows)])
+    send_lon(0, (0, levels), 0)
+    pack_weights(0)
+    for diagonal in (True, False):
+        send_columns(
+            lambda end, at: pack.at[0, end, 1:3, at, :],
+            lambda end, at: land_p.at[0, end, 1:3, at, :],
+            9,
+            diagonal,
+        )
+    for i in range(rows):
+        spread(2 + i, ids[2, OWN + i : OWN + i + 1])
+    drain_beside(recv_sem.at[5], 3 * rows)
+    own_edges(1)
+    drain_beside(recv_sem.at[7], 5 * rows)
+    push_lat()
     drain(recv_sem.at[4], 12)
-    got_columns(7, 5)
-    push_lat()
-    push_lon()
-    halo_slots()
-    got_columns(5, 3)
-    drain(recv_sem.at[3], border_rows)
-    drain(recv_sem.at[1], lon_rows)
-    lat_edges(1)
-
-    def middle(level, carry):
-        x_ref[level] = lon_level(1, level)
-        return carry
-
-    lax.fori_loop(0, levels, middle, 0, unroll=True)
-    regions(1, 2, [x_ref[0] * cos_ref[my_lat]])
+    push_lon(0)
+    for i in (0, 1, rows + 2, rows + 3):
+        spread(i, ids[2, OWN - 2 + i : OWN - 1 + i])
+    drain_beside(recv_sem.at[8], 12)
+    push_lon(1)
+    side_slots()
+    drain_beside(recv_sem.at[6], 12)
+    for part, slot in ((0, 1), (1, 3)):
+        drain(recv_sem.at[slot], border[part] + 4 * (parts[part][1] - parts[part][0]))
+        if part == 0:
+            terms = far_terms(1)
+        edges_and_lon(1, x_ref, terms, parts[part])
     solve(0)
     lat_rows(0)
-    send_columns(
-        lambda end, at: pack.at[0, end, 0, at, :], lambda end, at: land_p.at[0, end, 0, at, :], 9
-    )
-    send_border(0)
+    for diagonal in (True, False):
+        send_columns(
+            lambda end, at: pack.at[0, end, 0, at, :],
+            lambda end, at: land_p.at[0, end, 0, at, :],
+            9,
+            diagonal,
+        )
+    send_border(0, 0, 2)
+    send_border(0, 1, 11)
     push_totals()
     lax.fori_loop(1, count, scatter, 0)
     land[me] = send_ref[group_of(me)]
@@ -573,41 +627,28 @@
     got(7, blk * blk // lanes)
     covh[...] = covv[...].astype(jnp.bfloat16)
     covl[...] = (covv[...] - covh[...].astype(jnp.float32)).astype(jnp.bfloat16)
-    got_columns(9, 1)
-    drain(recv_sem.at[2], border_rows)
     drain(recv_sem.at[0], lon_rows)
-    lat_edges(0)
-
-    def last(level, carry):
-        out_ref[level] = lon_level(0, level)
-        return carry
-
-    lax.fori_loop(0, levels, last, 0, unroll=True)
+    drain_beside(recv_sem.at[9], 3 * rows)
+    own_edges(0)
+    drain_beside(recv_sem.at[10], 12)
+    for part, slot in ((0, 2), (1, 11)):
+        drain(recv_sem.at[slot], border[part])
+        if part == 0:
+            terms = far_terms(0)
+        edges_and_lon(0, out_ref, terms, parts[part])
     fetch(out_ref, out_h, 8)
     drain(send_sem.at[0], 2 * (border_rows + lon_rows) + 12)
-    for end in range(2):
-
-        @pl.when(send_if[end])
-        def _():
-            drain(send_sem.at[1 + end], 9 * column_rows)
-
+    drain_beside(send_sem.at[1], 9 * column_rows + 2 * rows)
     every = land.at[pl.ds(0, count - 1)]
     pltpu.make_async_copy(every, every, all_sem.at[0]).wait()
     pltpu.make_async_copy(every, every, all_sem.at[1]).wait()
     totals = jnp.sum(land[...], axis=0)
     coarse = totals.astype(jnp.bfloat16).astype(jnp.float32)
-    both = jnp.concatenate([coarse, totals - coarse, jnp.zeros((8, lanes), jnp.float32)], axis=0)
+    both = jnp.concatenate([coarse, totals - coarse, jnp.zeros((12, blk), jnp.float32)], axis=0)
     both = both.astype(jnp.bfloat16)
-    half = blk // 2
-
-    def product(at):
-        found = jnp.dot(both, covh[at], preferred_element_type=jnp.float32)
-        found = found + jnp.dot(both, covl[at], preferred_element_type=jnp.float32)
-        return found[:4] + found[4:8]
-
-    one, two = product(slice(0, half)), product(slice(half, blk))
-    for s in range(steps):
-        flux_ref[s : s + 1, :] = one[2 * s : 2 * s + 1] + two[2 * s + 1 : 2 * s + 2]
+    found = jnp.dot(both, covh[...], preferred_element_type=jnp.float32)
+    found = found + jnp.dot(both, covl[...], preferred_element_type=jnp.float32)
+    flux_ref[...] = found[:2] + found[2:4]
     fetch(flux_ref, flux_h, 8)
     got(8, levels * rows + steps * blk // lanes)
 
@@ -676,20 +717,20 @@
         vm((2, steps, 2 * levels + 8, lanes), f32),
         vm((2, steps, 2 * levels + 8, lanes), f32),
         vm((2, steps, 2, 2 * levels, lanes), f32),
-        vm((3, rows + 2 * OWN, lanes), f32),
-        vm((2, 3, rows + 2 * OWN, lanes), f32),
+        vm((5, rows + 2 * OWN, lanes), f32),
+        vm((2, 5, rows + 2 * OWN, lanes), f32),
         vm((2, 5, rows, lanes), f32),
         vm((2, 5, rows + 8, lanes), f32),
         vm((2, rows + 2 * OWN, lanes), f32),
-        vm((regions // 128, (rows + 5) * lanes), b16),
-        vm((128, (rows + 5) * lanes), b16),
-        vm((2 * (regions // 128), (rows + 5) * lanes), b16),
-        vm((regions // blk, 4, 128), f32),
-        vm((nlon * nlat, 4, 128), f32),
+        vm((2 * (regions // blk), (rows + 5) * lanes), b16),
+        vm((blk, (rows + 5) * lanes), b16),
+        vm((4 * (regions // blk), (rows + 5) * lanes), b16),
+        vm((regions // blk, 2, blk), f32),
+        vm((nlon * nlat, 2, blk), f32),
         vm((4 * levels * rows, lanes), f32),
         pltpu.SemaphoreType.DMA((9,)),
-        pltpu.SemaphoreType.DMA((3,)),
-        pltpu.SemaphoreType.DMA((11,)),
+        pltpu.SemaphoreType.DMA((2,)),
+        pltpu.SemaphoreType.DMA((12,)),
         pltpu.SemaphoreType.DMA((2,)),
     ]
     adjoint, flux = pl.pallas_call(

time: 19.3 us -> 18.7 us (0.969)
  Pallas kernels: 18.5 us -> 17.9 us
    pallas_call x1, Pallas kernels: 17.8 us -> 17.2 us  [per_device(): pl.pallas_call(functools.partial(kernel, nlon, nlat, width), out_shape=(p...]
where the time goes in v3:
time: 18.7 us; the launch traced here: 18.5 us
  Pallas kernels  17.9 us (96%)
  between operations  0.64 us (3%)
    pallas_call x1, Pallas kernels, per_device(): pl.pallas_call(functools.partial(kernel, nlon, nlat, width), out_shape=(p...  17.2 us
    pallas_call x1, Pallas kernels, per_device(): pl.pallas_call(store, out_shape=(jax.ShapeDtypeStruct(field, f32), jax.Sh...  0.73 us

profile of v3, /device:TPU:0, one launch (start us, length us, event | category | flops | bytes accessed | tf_op | source)
XLA Modules:
  0.0 18.5 jit_solution(5615095585182310428)
XLA Ops:
  0.6 17.2 %shard_map.113 = (f32[34,16,128]{2,1,0:T(8,128)S(1)}, f32[2,256]{1,0:T(2,128)S(1)}) custom-call(f32[34,16,128]{2,1,0:T(8,128)} %adj_h.1, f32[2,34,16,128]{3,2,1,0:T(8,128)} %lonc_h.1, s32[2,34,16,128]{3,2,1,0:T(8,128)} %lonb_h.1, f32[2,34,16,128]{3,2,1,0:T(8,128)} %latc_h.1, s32[2,34,16,128]{3,2,1,0:T(8,128)} %latb_h.1, f32[2,33,16,128]{3,2,1,0:T(8,128)} %mix_h.1, ...), custom_call_target="tpu_custom_call" | custom-call | tf_op jit(solution)/shard_map/pallas_call | solution.py:736
  17.8 0.7 %shard_map.114 = (f32[34,16,128]{2,1,0:T(8,128)}, f32[2,256]{1,0:T(2,128)}) custom-call(f32[34,16,128]{2,1,0:T(8,128)S(1)} %get-tuple-element.4.adjoint_v, f32[2,256]{1,0:T(2,128)S(1)} %get-tuple-element.5.flux_v), custom_call_target="tpu_custom_call" | custom-call | tf_op jit(solution)/shard_map/pallas_call | solution.py:763

commit v4 on v3

--- a/solution.py
+++ b/solution.py
@@ -42,9 +42,9 @@
     order_h,
     cos_h,
     out_h,
-    flux_h,
+    land,
+    covv,
     out_ref,
-    flux_ref,
     rmap_ref,
     order_ref,
     cos_ref,
@@ -54,12 +54,10 @@
     latb,
     lonc,
     lonb,
-    covv,
-    covh,
-    covl,
     inv_ref,
     kin_ref,
     nr_ref,
+    join_ref,
     y_ref,
     ext,
     lw,
@@ -69,6 +67,8 @@
     rows_a,
     far_a,
     rows_w,
+    rows_c,
+    delta,
     ids,
     beside,
     lat_c,
@@ -78,7 +78,6 @@
     cht,
     amat,
     send_ref,
-    land,
     sizer,
     local_sem,
     send_sem,
@@ -158,51 +157,72 @@
     east = (lax.rem(my_lon + 1, nlon), my_lat)
     west = (lax.rem(my_lon + nlon - 1, nlon), my_lat)
 
+    meet = levels // 2
+
     def coefficients(s):
-        k = mixv[s, 0]
-        inv = 1.0 / (1.0 + k)
-        inv_ref[s, 0] = inv
-        kin_ref[s, 0] = zero
-        nr_ref[s, 0] = k * inv
-
-        def body(level, ahead):
-            lower, k = mixv[s, level - 1], mixv[s, level]
-            inv = 1.0 / ((1.0 + k) + lower * (1.0 - ahead))
-            inv_ref[s, level] = inv
-            kin_ref[s, level] = lower * inv
-            ahead = k * inv
-            nr_ref[s, level] = ahead
+        def sweep(order, before, after):
+            ahead = None
+            for level in order:
+                inner, outer = before(level), after(level)
+                if ahead is None:
+                    inv = 1.0 / (1.0 + outer)
+                    kin_ref[s, level] = zero
+                else:
+                    inv = 1.0 / ((1.0 + outer) + inner * (1.0 - ahead))
+                    kin_ref[s, level] = inner * inv
+                inv_ref[s, level] = inv
+                ahead = outer * inv
+                nr_ref[s, level] = ahead
             return ahead
 
-        ahead = lax.fori_loop(1, levels - 1, body, k * inv, unroll=True)
-        lower = mixv[s, levels - 2]
-        inv = 1.0 / (1.0 + lower * (1.0 - ahead))
-        inv_ref[s, levels - 1] = inv
-        kin_ref[s, levels - 1] = lower * inv
-        nr_ref[s, levels - 1] = zero
+        def below(level):
+            return mixv[s, level - 1] if level > 0 else None
+
+        def above(level):
+            return mixv[s, level] if level < levels - 1 else None
+
+        up = sweep(range(meet), below, above)
+        down = sweep(range(levels - 1, meet - 1, -1), above, below)
+        join_ref[s] = 1.0 / (1.0 - up * down)
 
     def tail_head(value, level, tail, head):
         turned = roll(value, 2 * level + 2)
         return jnp.where(pair == level, turned, tail), jnp.where(pair == level + 1, turned, head)
 
     def solve(s):
-        def up(level, carried):
-            carried = x_ref[level] * inv_ref[s, level] + kin_ref[s, level] * carried
-            y_ref[level] = carried
-            return carried
-
-        lax.fori_loop(0, levels, up, zero, unroll=True)
-
-        def down(i, carry):
-            value, tail, head = carry
+        def carry(level, carried):
+            value = x_ref[level] * inv_ref[s, level]
+            return value if carried is None else value + kin_ref[s, level] * carried
+
+        up = down = None
+        for i in range(levels - meet):
+            if i < meet:
+                up = carry(i, up)
+                y_ref[i] = up
             level = levels - 1 - i
-            value = y_ref[level] + nr_ref[s, level] * value
-            y_ref[level] = value
-            raw_rows[0, pl.ds(2 * level, 2), :] = value[rows - 2 :]
-            raw_rows[1, pl.ds(2 * level, 2), :] = value[:2]
-            return (value,) + tail_head(value, level, tail, head)
-
-        _, tail, head = lax.fori_loop(0, levels, down, (zero, zero, zero), unroll=True)
+            down = carry(level, down)
+            y_ref[level] = down
+        tail = head = zero
+        up_value = down_value = None
+        for i in range(levels - meet):
+            level = meet + i
+            if i == 0:
+                down_value = (down + nr_ref[s, level] * up) * join_ref[s]
+            else:
+                down_value = y_ref[level] + nr_ref[s, level] * down_value
+            found = [(level, down_value)]
+            if i < meet:
+                level = meet - 1 - i
+                if i == 0:
+                    up_value = up + nr_ref[s, level] * down_value
+                else:
+                    up_value = y_ref[level] + nr_ref[s, level] * up_value
+                found.append((level, up_value))
+            for level, value in found:
+                y_ref[level] = value
+                raw_rows[0, pl.ds(2 * level, 2), :] = value[rows - 2 :]
+                raw_rows[1, pl.ds(2 * level, 2), :] = value[:2]
+                tail, head = tail_head(value, level, tail, head)
         head = roll(head, lanes - 2)
         for member, value in enumerate((tail, head)):
             pack[s, member, 0, OWN : OWN + rows] = value
@@ -231,11 +251,25 @@
             rows_a[0, s, at : at + 2] = found[1][member][rows - 2 :]
             rows_a[1, s, at : at + 2] = found[1][member][:2]
 
+    def row_weights(s):
+        lane = lax.broadcasted_iota(jnp.int32, (2 * levels, lanes), 1)
+        for side in range(2):
+            m2, m1, m0, p1 = face_weights(rows_w[side, s, 0], rows_w[side, s, 1])
+            ahead1 = jnp.where(lane <= lanes - 2, roll(m1, lanes - 1), 0.0)
+            ahead2 = jnp.where(lane <= lanes - 3, roll(m2, lanes - 2), 0.0)
+            here = jnp.where(lane >= 1, m0, 0.0)
+            behind = jnp.where(lane >= 2, roll(p1, 1), 0.0)
+            found = (1.0 - ahead1 + here, ahead1 - ahead2, ahead2, behind - here, -behind)
+            for k, value in enumerate(found):
+                rows_c[side, k] = value
+
     def lat_rows(s):
         for side in range(2):
-            rows_a[side, s, 8:] = lat_pass(
-                raw_rows[side], rows_w[side, s, 0], rows_w[side, s, 1]
-            )
+            a = raw_rows[side]
+            value = rows_c[side, 0] * a
+            for k, turn in ((1, lanes - 1), (2, lanes - 2), (3, 1), (4, 2)):
+                value = value + rows_c[side, k] * roll(a, turn)
+            rows_a[side, s, 8:] = value
 
     def lat_pass(a, courant, branch):
         at = lax.broadcasted_iota(jnp.int32, a.shape, 1)
@@ -263,40 +297,67 @@
         _, _, m0_head, p1_head = face_weights(pack[s, 1, 1, at], pack[s, 1, 2, at])
         _, _, _, p1_before = face_weights(land_p[s, 0, 1, at], land_p[s, 0, 2, at])
         jump = after - jnp.where(even, roll(tail, lanes - 1), roll(after, 1))
-        top = m2_after * jump + roll(jnp.where(even, m1_after * jump, 0.0), 1)
-        top = jnp.where(my_lat < nlat - 1, top, 0.0)
+        top_here = jnp.where(has_north, m2_after * jump, 0.0)
+        top_next = jnp.where(jnp.logical_and(even, has_north), m1_after * jump, 0.0)
         jump = jnp.where(even, head - roll(before, lanes - 1), before - roll(before, 1))
-        flux = jnp.where(even, p1_head, p1_before) * jump
-        low = jnp.where(even, m0_head * jump + roll(flux, lanes - 1), roll(flux, 1))
-        low = roll(jnp.where(my_lat > 0, low, 0.0), 2)
-        first = lax.rem(lane, 4) < 2
-        both = (jnp.where(first, top, low), jnp.where(first, low, top))
+        flux = jnp.where(has_south, jnp.where(even, p1_head, p1_before) * jump, 0.0)
+        low_here = jnp.where(has_south, m0_head * jump, 0.0)
         edge = jnp.logical_or(lane < 2, lane >= lanes - 2)
 
-        def at_level(level):
-            return jnp.where(edge, roll(both[level % 2], lanes - 2 - 2 * level), 0.0)
-
-        return at_level
+        def turned_back(by):
+            def turn(value, shift):
+                shift = (shift - by) % lanes
+                return roll(value, shift) if shift else value
+
+            first = lax.rem(lane + by, 4) < 2
+            evens = lax.rem(lane + by, 2) == 0
+            top = turn(top_here, 0) + turn(top_next, 1)
+            low = jnp.where(evens, turn(low_here, 2) + turn(flux, 1), turn(flux, 3))
+            return jnp.where(first, top, low), jnp.where(first, low, top)
+
+        return turned_back, edge
 
     def own_edges(s):
-        terms = edge_terms(s, slice(OWN, OWN + rows))
+        turned_back, edge = edge_terms(s, slice(OWN, OWN + rows))
+        both = turned_back(0)
         for level in range(levels):
-            ext[s, level, OWN : OWN + rows] += terms(level)
-
-    def far_terms(s):
-        for side, where in enumerate((slice(OWN - 2, OWN), slice(OWN + rows, OWN + rows + 2))):
+            turned = roll(both[level % 2], lanes - 2 - 2 * level)
+            ext[s, level, OWN : OWN + rows] += jnp.where(edge, turned, 0.0)
+
+    def far_edges(s):
+        end = OWN + rows
+        for side, where in enumerate((slice(OWN - 2, OWN), slice(end, end + 2))):
             for member in range(2):
                 pack[s, member, 0, where] = far_a[side, s, 2 * member : 2 * member + 2]
                 far = 4 + 2 * member
                 pack[s, 1, 1 + member, where] = far_a[side, s, far : far + 2]
-        return edge_terms(s, slice(0, OWN)), edge_terms(s, slice(OWN + rows, 2 * OWN + rows))
-
-    def edges_and_lon(s, target, terms, part):
+        down = lax.broadcasted_iota(jnp.int32, (8, lanes), 0)
+        for side, (at, row) in enumerate(((slice(0, OWN), OWN - 2), (slice(end, end + OWN), 0))):
+            turned_back, edge = edge_terms(s, at)
+            both = turned_back(0), turned_back(1)
+            rows2 = [
+                jnp.where(
+                    lax.rem(down // 2 + levels - 1, 2) == 0,
+                    jnp.broadcast_to(both[odd][0][row + odd : row + odd + 1], (8, lanes)),
+                    jnp.broadcast_to(both[odd][1][row + odd : row + odd + 1], (8, lanes)),
+                )
+                for odd in range(2)
+            ]
+            tile = jnp.where(lax.rem(down, 2) == 0, rows2[0], rows2[1])
+            for v in range((2 * levels + 7) // 8):
+                turn = (8 * v - 2 * levels) % lanes
+                late = turn > lanes - 8
+                source = roll(tile, lanes // 2) if late else tile
+                turn = turn - lanes // 2 if late else turn
+                turned = pltpu.roll(source, turn, 1, stride=1, stride_axis=0)
+                delta[side, 8 * v : 8 * v + 8] = jnp.where(edge, turned, 0.0)
+
+    def edges_and_lon(s, target, part):
         end = OWN + rows
         for level in range(*part):
-            two = slice(8 + 2 * level, 10 + 2 * level)
-            ext[s, level, OWN - 2 : OWN] = far_a[0, s, two] + terms[0](level)[OWN - 2 :]
-            ext[s, level, end : end + 2] = far_a[1, s, two] + terms[1](level)[:2]
+            far, two = slice(8 + 2 * level, 10 + 2 * level), slice(2 * (levels - 1 - level), 2 * (levels - level))
+            ext[s, level, OWN - 2 : OWN] = far_a[0, s, far] + delta[0, two]
+            ext[s, level, end : end + 2] = far_a[1, s, far] + delta[1, two]
         for level in range(*part):
             target[level] = lon_level(s, level)
 
@@ -472,6 +533,7 @@
     solve(1)
     got(2, 2 * levels * rows)
     pack_weights(1)
+    row_weights(1)
     lat_rows(1)
     got(3, 2 * levels * rows)
     lon_own_weights(1)
@@ -583,6 +645,7 @@
     lon_own_weights(0)
     send_lon(0, (0, levels), 0)
     pack_weights(0)
+    row_weights(0)
     for diagonal in (True, False):
         send_columns(
             lambda end, at: pack.at[0, end, 1:3, at, :],
@@ -607,8 +670,8 @@
     for part, slot in ((0, 1), (1, 3)):
         drain(recv_sem.at[slot], border[part] + 4 * (parts[part][1] - parts[part][0]))
         if part == 0:
-            terms = far_terms(1)
-        edges_and_lon(1, x_ref, terms, parts[part])
+            far_edges(1)
+        edges_and_lon(1, x_ref, parts[part])
     solve(0)
     lat_rows(0)
     for diagonal in (True, False):
@@ -622,11 +685,9 @@
     send_border(0, 1, 11)
     push_totals()
     lax.fori_loop(1, count, scatter, 0)
-    land[me] = send_ref[group_of(me)]
+    fetch(send_ref.at[group_of(me)], land.at[me], 8)
     lat_inner(0)
     got(7, blk * blk // lanes)
-    covh[...] = covv[...].astype(jnp.bfloat16)
-    covl[...] = (covv[...] - covh[...].astype(jnp.float32)).astype(jnp.bfloat16)
     drain(recv_sem.at[0], lon_rows)
     drain_beside(recv_sem.at[9], 3 * rows)
     own_edges(0)
@@ -634,34 +695,33 @@
     for part, slot in ((0, 2), (1, 11)):
         drain(recv_sem.at[slot], border[part])
         if part == 0:
-            terms = far_terms(0)
-        edges_and_lon(0, out_ref, terms, parts[part])
+            far_edges(0)
+        edges_and_lon(0, out_ref, parts[part])
     fetch(out_ref, out_h, 8)
+    got(8, levels * rows + 2 * blk // lanes)
     drain(send_sem.at[0], 2 * (border_rows + lon_rows) + 12)
     drain_beside(send_sem.at[1], 9 * column_rows + 2 * rows)
     every = land.at[pl.ds(0, count - 1)]
     pltpu.make_async_copy(every, every, all_sem.at[0]).wait()
     pltpu.make_async_copy(every, every, all_sem.at[1]).wait()
+
+
+def finish(adjoint_v, land, cov, adjoint_h, flux_h, flux, sem):
+    whole = pltpu.make_async_copy(adjoint_v, adjoint_h, sem.at[0])
+    whole.start()
     totals = jnp.sum(land[...], axis=0)
     coarse = totals.astype(jnp.bfloat16).astype(jnp.float32)
-    both = jnp.concatenate([coarse, totals - coarse, jnp.zeros((12, blk), jnp.float32)], axis=0)
-    both = both.astype(jnp.bfloat16)
-    found = jnp.dot(both, covh[...], preferred_element_type=jnp.float32)
-    found = found + jnp.dot(both, covl[...], preferred_element_type=jnp.float32)
-    flux_ref[...] = found[:2] + found[2:4]
-    fetch(flux_ref, flux_h, 8)
-    got(8, levels * rows + steps * blk // lanes)
-
-
-def store(adjoint_v, flux_v, adjoint_h, flux_h, sem):
-    copies = (
-        pltpu.make_async_copy(adjoint_v, adjoint_h, sem.at[0]),
-        pltpu.make_async_copy(flux_v, flux_h, sem.at[1]),
-    )
-    for copy in copies:
-        copy.start()
-    for copy in copies:
-        copy.wait()
+    rest = jnp.zeros((12, totals.shape[1]), jnp.float32)
+    both = jnp.concatenate([coarse, totals - coarse, rest], axis=0).astype(jnp.bfloat16)
+    cov_high = cov[...].astype(jnp.bfloat16)
+    cov_low = (cov[...] - cov_high.astype(jnp.float32)).astype(jnp.bfloat16)
+    found = jnp.dot(both, cov_high, preferred_element_type=jnp.float32)
+    found = found + jnp.dot(both, cov_low, preferred_element_type=jnp.float32)
+    flux[...] = found[:2] + found[2:4]
+    part = pltpu.make_async_copy(flux, flux_h, sem.at[1])
+    part.start()
+    part.wait()
+    whole.wait()
 
 
 def per_device(
@@ -692,7 +752,6 @@
     vm = pltpu.VMEM
     scratch = [
         vm(field, f32),
-        vm((steps, blk), f32),
         vm((rows, lanes), i32),
         vm((regions // 128, 128), i32),
         vm((nlat, 1, lanes), f32),
@@ -702,12 +761,10 @@
         vm((steps,) + field, i32),
         vm((steps,) + field, f32),
         vm((steps,) + field, i32),
-        vm((blk, blk), f32),
-        vm((blk, blk), b16),
-        vm((blk, blk), b16),
         vm((steps,) + field, f32),
         vm((steps,) + field, f32),
         vm((steps,) + field, f32),
+        vm((steps, rows, lanes), f32),
         vm(field, f32),
         vm((steps,) + tall, f32),
         vm((steps, 4) + tall, f32),
@@ -717,6 +774,8 @@
         vm((2, steps, 2 * levels + 8, lanes), f32),
         vm((2, steps, 2 * levels + 8, lanes), f32),
         vm((2, steps, 2, 2 * levels, lanes), f32),
+        vm((2, 5, 2 * levels, lanes), f32),
+        vm((2, 2 * levels + 8, lanes), f32),
         vm((5, rows + 2 * OWN, lanes), f32),
         vm((2, 5, rows + 2 * OWN, lanes), f32),
         vm((2, 5, rows, lanes), f32),
@@ -726,24 +785,21 @@
         vm((blk, (rows + 5) * lanes), b16),
         vm((4 * (regions // blk), (rows + 5) * lanes), b16),
         vm((regions // blk, 2, blk), f32),
-        vm((nlon * nlat, 2, blk), f32),
         vm((4 * levels * rows, lanes), f32),
         pltpu.SemaphoreType.DMA((9,)),
         pltpu.SemaphoreType.DMA((2,)),
         pltpu.SemaphoreType.DMA((12,)),
         pltpu.SemaphoreType.DMA((2,)),
     ]
-    adjoint, flux = pl.pallas_call(
+    adjoint, landed, cov = pl.pallas_call(
         functools.partial(kernel, nlon, nlat, width),
         out_shape=(
             pltpu.VMEM(field, f32),
-            pltpu.VMEM((steps, blk), f32),
+            pltpu.VMEM((nlon * nlat, steps, blk), f32),
+            pltpu.VMEM((blk, blk), f32),
         ),
         in_specs=[pl.BlockSpec(memory_space=pltpu.HBM)] * 10,
-        out_specs=(
-            pl.BlockSpec(memory_space=pl.ANY),
-            pl.BlockSpec(memory_space=pl.ANY),
-        ),
+        out_specs=(pl.BlockSpec(memory_space=pl.ANY),) * 3,
         scratch_shapes=scratch,
         compiler_params=pltpu.CompilerParams(
             collective_id=0, has_side_effects=True, vmem_limit_bytes=61 * 1024 * 1024
@@ -761,15 +817,19 @@
         cosines,
     )
     adjoint, flux = pl.pallas_call(
-        store,
+        finish,
         out_shape=(
             jax.ShapeDtypeStruct(field, f32),
             jax.ShapeDtypeStruct((steps, blk), f32),
         ),
-        in_specs=[pl.BlockSpec(memory_space=pl.ANY)] * 2,
+        in_specs=[
+            pl.BlockSpec(memory_space=pl.ANY),
+            pl.BlockSpec(memory_space=pltpu.VMEM),
+            pl.BlockSpec(memory_space=pltpu.VMEM),
+        ],
         out_specs=(pl.BlockSpec(memory_space=pl.ANY),) * 2,
-        scratch_shapes=[pltpu.SemaphoreType.DMA((2,))],
-    )(pltpu.with_memory_space_constraint(adjoint, pltpu.VMEM), pltpu.with_memory_space_constraint(flux, pltpu.VMEM))
+        scratch_shapes=[vm((steps, blk), f32), pltpu.SemaphoreType.DMA((2,))],
+    )(*(pltpu.with_memory_space_constraint(x, pltpu.VMEM) for x in (adjoint, landed, cov)))
     if width < blk:
         start = lax.rem(lax.axis_index("lat") * width, blk)
         flux = lax.dynamic_slice_in_dim(flux, start, width, 1)

time: 18.7 us -> 18.5 us (0.989)
  Pallas kernels: 17.9 us -> 17.7 us
    pallas_call x1, Pallas kernels: 17.2 us -> 16.9 us  [per_device(): pl.pallas_call(functools.partial(kernel, nlon, nlat, width), out_shape=(p...]
where the time goes in v4:
time: 18.5 us; the launch traced here: 18.4 us
  Pallas kernels  17.7 us (96%)
  between operations  0.64 us (3%)
    pallas_call x1, Pallas kernels, per_device(): pl.pallas_call(functools.partial(kernel, nlon, nlat, width), out_shape=(p...  16.9 us
    pallas_call x1, Pallas kernels, per_device(): pl.pallas_call(finish, out_shape=(jax.ShapeDtypeStruct(field, f32), jax.S...  0.79 us

profile of v4, /device:TPU:0, one launch (start us, length us, event | category | flops | bytes accessed | tf_op | source)
XLA Modules:
  0.0 18.4 jit_solution(4203023901770167325)
XLA Ops:
  0.6 16.9 %shard_map.113 = (f32[34,16,128]{2,1,0:T(8,128)S(1)}, f32[32,2,256]{2,1,0:T(2,128)S(1)}, f32[256,256]{1,0:T(8,128)S(1)}) custom-call(f32[34,16,128]{2,1,0:T(8,128)} %adj_h.1, f32[2,34,16,128]{3,2,1,0:T(8,128)} %lonc_h.1, s32[2,34,16,128]{3,2,1,0:T(8,128)} %lonb_h.1, f32[2,34,16,128]{3,2,1,0:T(8,128)} %latc_h.1, s32[2,34,16,128]{3,2,1,0:T(8,128)} %latb_h.1, ...), custom_call_target="tpu_custom_call" | custom-call | tf_op jit(solution)/shard_map/pallas_call | solution.py:794
  17.6 0.8 %shard_map.114 = (f32[34,16,128]{2,1,0:T(8,128)}, f32[2,256]{1,0:T(2,128)}) custom-call(f32[34,16,128]{2,1,0:T(8,128)S(1)} %get-tuple-element.5.adjoint_v, f32[32,2,256]{2,1,0:T(2,128)S(1)} %get-tuple-element.6.land, f32[256,256]{1,0:T(8,128)S(1)} %get-tuple-element.7.cov), custom_call_target="tpu_custom_call" | custom-call | tf_op jit(solution)/shard_map/pallas_call | solution.py:819

commit v5 on v4

--- a/solution.py
+++ b/solution.py
@@ -121,17 +121,17 @@
     fetch(adj_h, x_ref, 1)
     fetch(latc_h.at[1], latc.at[1], 2)
     fetch(latb_h.at[1], latb.at[1], 2)
-    fetch(lonc_h.at[1], lonc.at[1], 3)
-    fetch(lonb_h.at[1], lonb.at[1], 3)
-    fetch(latc_h.at[0], latc.at[0], 4)
-    fetch(latb_h.at[0], latb.at[0], 4)
-    fetch(lonc_h.at[0], lonc.at[0], 4)
-    fetch(lonb_h.at[0], lonb.at[0], 4)
-    fetch(rmap_h, rmap_ref, 5)
-    fetch(order_h, order_ref, 5)
-    fetch(cos_h, cos_ref, 5)
-    fetch(mix_h.at[0], mixv.at[0], 6)
-    fetch(cov_h.at[(my_lat * width) // blk], covv, 7)
+    fetch(lonc_h.at[1], lonc.at[1], 2)
+    fetch(lonb_h.at[1], lonb.at[1], 2)
+    fetch(latc_h.at[0], latc.at[0], 3)
+    fetch(latb_h.at[0], latb.at[0], 3)
+    fetch(lonc_h.at[0], lonc.at[0], 3)
+    fetch(lonb_h.at[0], lonb.at[0], 3)
+    fetch(rmap_h, rmap_ref, 3)
+    fetch(order_h, order_ref, 3)
+    fetch(cos_h, cos_ref, 3)
+    fetch(mix_h.at[0], mixv.at[0], 4)
+    fetch(cov_h.at[(my_lat * width) // blk], covv, 4)
     lax.fori_loop(count // 4, count, greet, 0)
 
     lane = lax.broadcasted_iota(jnp.int32, (rows, lanes), 1)
@@ -531,14 +531,12 @@
     coefficients(1)
     got(1, levels * rows)
     solve(1)
-    got(2, 2 * levels * rows)
+    got(2, 4 * levels * rows)
     pack_weights(1)
     row_weights(1)
     lat_rows(1)
-    got(3, 2 * levels * rows)
     lon_own_weights(1)
-    got(4, 4 * levels * rows)
-    got(5, rows + order_ref.shape[0] + nlat)
+    got(3, 4 * levels * rows + rows + order_ref.shape[0] + nlat)
     ids[0, OWN : OWN + rows] = lonc[0, 0]
     ids[1, OWN : OWN + rows] = lonb[0, 0].astype(jnp.float32)
     ids[3, OWN : OWN + rows] = latc[0, 0]
@@ -623,24 +621,23 @@
             send_columns(
                 lambda end, at: ids.at[three, at, :],
                 lambda end, at: beside.at[end, three, at, :],
-                7,
+                5,
                 True,
             )
         else:
             send_columns(
-                lambda end, at: ids.at[:, at, :], lambda end, at: beside.at[end, :, at, :], 7, False
+                lambda end, at: ids.at[:, at, :], lambda end, at: beside.at[end, :, at, :], 5, False
             )
 
     send_packs(True)
     remote(ids.at[three, last_two, :], ids.at[three, low, :], 0, 4, east)
     remote(ids.at[three, first, :], ids.at[three, high, :], 0, 4, west)
+    send_packs(False)
     for part, slot in ((0, 1), (1, 3)):
         send_border(1, part, slot)
-        if part == 0:
-            send_packs(False)
         send_lon(1, parts[part], slot)
     lat_inner(1)
-    got(6, (levels - 1) * rows)
+    got(4, (levels - 1) * rows + blk * blk // lanes)
     coefficients(0)
     lon_own_weights(0)
     send_lon(0, (0, levels), 0)
@@ -650,27 +647,26 @@
         send_columns(
             lambda end, at: pack.at[0, end, 1:3, at, :],
             lambda end, at: land_p.at[0, end, 1:3, at, :],
-            9,
+            8,
             diagonal,
         )
     for i in range(rows):
         spread(2 + i, ids[2, OWN + i : OWN + i + 1])
-    drain_beside(recv_sem.at[5], 3 * rows)
+    drain_beside(recv_sem.at[5], 8 * rows)
     own_edges(1)
-    drain_beside(recv_sem.at[7], 5 * rows)
     push_lat()
     drain(recv_sem.at[4], 12)
     push_lon(0)
     for i in (0, 1, rows + 2, rows + 3):
         spread(i, ids[2, OWN - 2 + i : OWN - 1 + i])
-    drain_beside(recv_sem.at[8], 12)
-    push_lon(1)
-    side_slots()
-    drain_beside(recv_sem.at[6], 12)
+    drain_beside(recv_sem.at[6], 24)
     for part, slot in ((0, 1), (1, 3)):
         drain(recv_sem.at[slot], border[part] + 4 * (parts[part][1] - parts[part][0]))
         if part == 0:
             far_edges(1)
+        else:
+            push_lon(1)
+            side_slots()
         edges_and_lon(1, x_ref, parts[part])
     solve(0)
     lat_rows(0)
@@ -678,27 +674,26 @@
         send_columns(
             lambda end, at: pack.at[0, end, 0, at, :],
             lambda end, at: land_p.at[0, end, 0, at, :],
-            9,
+            8,
             diagonal,
         )
     send_border(0, 0, 2)
-    send_border(0, 1, 11)
+    send_border(0, 1, 7)
     push_totals()
     lax.fori_loop(1, count, scatter, 0)
-    fetch(send_ref.at[group_of(me)], land.at[me], 8)
+    fetch(send_ref.at[group_of(me)], land.at[me], 5)
     lat_inner(0)
-    got(7, blk * blk // lanes)
     drain(recv_sem.at[0], lon_rows)
-    drain_beside(recv_sem.at[9], 3 * rows)
+    drain_beside(recv_sem.at[8], 3 * rows)
     own_edges(0)
-    drain_beside(recv_sem.at[10], 12)
-    for part, slot in ((0, 2), (1, 11)):
+    drain_beside(recv_sem.at[9], 12)
+    for part, slot in ((0, 2), (1, 7)):
         drain(recv_sem.at[slot], border[part])
         if part == 0:
             far_edges(0)
         edges_and_lon(0, out_ref, parts[part])
-    fetch(out_ref, out_h, 8)
-    got(8, levels * rows + 2 * blk // lanes)
+    fetch(out_ref, out_h, 5)
+    got(5, levels * rows + 2 * blk // lanes)
     drain(send_sem.at[0], 2 * (border_rows + lon_rows) + 12)
     drain_beside(send_sem.at[1], 9 * column_rows + 2 * rows)
     every = land.at[pl.ds(0, count - 1)]
@@ -785,10 +780,10 @@
         vm((blk, (rows + 5) * lanes), b16),
         vm((4 * (regions // blk), (rows + 5) * lanes), b16),
         vm((regions // blk, 2, blk), f32),
-        vm((4 * levels * rows, lanes), f32),
-        pltpu.SemaphoreType.DMA((9,)),
+        vm((5 * levels * rows, lanes), f32),
+        pltpu.SemaphoreType.DMA((6,)),
         pltpu.SemaphoreType.DMA((2,)),
-        pltpu.SemaphoreType.DMA((12,)),
+        pltpu.SemaphoreType.DMA((10,)),
         pltpu.SemaphoreType.DMA((2,)),
     ]
     adjoint, landed, cov = pl.pallas_call(

time: 18.5 us -> 18.3 us (0.989)
  Pallas kernels: 17.7 us -> 17.5 us
    pallas_call x1, Pallas kernels: 16.9 us -> 16.7 us  [per_device(): pl.pallas_call(functools.partial(kernel, nlon, nlat, width), out_shape=(p...]
where the time goes in v5:
time: 18.3 us; the launch traced here: 18.1 us
  Pallas kernels  17.5 us (96%)
  between operations  0.64 us (3%)
    pallas_call x1, Pallas kernels, per_device(): pl.pallas_call(functools.partial(kernel, nlon, nlat, width), out_shape=(p...  16.7 us
    pallas_call x1, Pallas kernels, per_device(): pl.pallas_call(finish, out_shape=(jax.ShapeDtypeStruct(field, f32), jax.S...  0.79 us

profile of v5, /device:TPU:0, one launch (start us, length us, event | category | flops | bytes accessed | tf_op | source)
XLA Modules:
  0.0 18.1 jit_solution(10916436800157149849)
XLA Ops:
  0.6 16.7 %shard_map.113 = (f32[34,16,128]{2,1,0:T(8,128)S(1)}, f32[32,2,256]{2,1,0:T(2,128)S(1)}, f32[256,256]{1,0:T(8,128)S(1)}) custom-call(f32[34,16,128]{2,1,0:T(8,128)} %adj_h.1, f32[2,34,16,128]{3,2,1,0:T(8,128)} %lonc_h.1, s32[2,34,16,128]{3,2,1,0:T(8,128)} %lonb_h.1, f32[2,34,16,128]{3,2,1,0:T(8,128)} %latc_h.1, s32[2,34,16,128]{3,2,1,0:T(8,128)} %latb_h.1, ...), custom_call_target="tpu_custom_call" | custom-call | tf_op jit(solution)/shard_map/pallas_call | solution.py:789
  17.4 0.8 %shard_map.114 = (f32[34,16,128]{2,1,0:T(8,128)}, f32[2,256]{1,0:T(2,128)}) custom-call(f32[34,16,128]{2,1,0:T(8,128)S(1)} %get-tuple-element.5.adjoint_v, f32[32,2,256]{2,1,0:T(2,128)S(1)} %get-tuple-element.6.land, f32[256,256]{1,0:T(8,128)S(1)} %get-tuple-element.7.cov), custom_call_target="tpu_custom_call" | custom-call | tf_op jit(solution)/shard_map/pallas_call | solution.py:814

commit v6 on v5

--- a/solution.py
+++ b/solution.py
@@ -553,34 +553,43 @@
     send_if, recv_if = (has_north, has_south), (has_south, has_north)
     column_rows = rows + 4
 
+    def send_end(source, target, recv_base, diagonal, end, lat):
+        for lon, src, dst in (
+            ((turn[1], last_two, low), (turn[-1], first, high))
+            if diagonal
+            else ((my_lon, own_rows, own_rows),)
+        ):
+            remote(
+                source(end, src),
+                target(end, dst),
+                1,
+                recv_base + (1 if diagonal else 0),
+                (lon, lat),
+            )
+
     def send_columns(source, target, recv_base, diagonal):
+        if nlat == 2:
+            send_end(source, target, recv_base, diagonal, my_lat, 1 - my_lat)
+            return
         for end in range(2):
 
             @pl.when(send_if[end])
             def _():
-                for lon, src, dst in (
-                    ((turn[1], last_two, low), (turn[-1], first, high))
-                    if diagonal
-                    else ((my_lon, own_rows, own_rows),)
-                ):
-                    remote(
-                        source(end, src),
-                        target(end, dst),
-                        1,
-                        recv_base + (1 if diagonal else 0),
-                        (lon, toward[end]),
-                    )
+                send_end(source, target, recv_base, diagonal, end, toward[end])
 
     beside_count = jnp.where(has_north, 1, 0) + jnp.where(has_south, 1, 0)
 
     def drain_beside(sem, count_rows):
+        if nlat == 2:
+            drain(sem, count_rows)
+            return
         for ends in (1, 2):
 
             @pl.when(beside_count == ends)
             def _():
                 drain(sem, ends * count_rows)
 
-    half = levels // 2
+    half = 2 * levels // 3
     parts = ((0, half), (half, levels))
     spans = (pl.ds(0, 8 + 2 * half), pl.ds(8 + 2 * half, 2 * (levels - half)))
     border = (2 * (8 + 2 * half), 4 * (levels - half))

time: 18.3 us -> 18.2 us (level)
  no operation moved by 1% of the time
where the time goes in v6:
time: 18.2 us; the launch traced here: 18.1 us
  Pallas kernels  17.4 us (96%)
  between operations  0.64 us (4%)
    pallas_call x1, Pallas kernels, per_device(): pl.pallas_call(functools.partial(kernel, nlon, nlat, width), out_shape=(p...  16.6 us
    pallas_call x1, Pallas kernels, per_device(): pl.pallas_call(finish, out_shape=(jax.ShapeDtypeStruct(field, f32), jax.S...  0.79 us

profile of v6, /device:TPU:0, one launch (start us, length us, event | category | flops | bytes accessed | tf_op | source)
XLA Modules:
  0.0 18.1 jit_solution(12032658533941023940)
XLA Ops:
  0.6 16.6 %shard_map.113 = (f32[34,16,128]{2,1,0:T(8,128)S(1)}, f32[32,2,256]{2,1,0:T(2,128)S(1)}, f32[256,256]{1,0:T(8,128)S(1)}) custom-call(f32[34,16,128]{2,1,0:T(8,128)} %adj_h.1, f32[2,34,16,128]{3,2,1,0:T(8,128)} %lonc_h.1, s32[2,34,16,128]{3,2,1,0:T(8,128)} %lonb_h.1, f32[2,34,16,128]{3,2,1,0:T(8,128)} %latc_h.1, s32[2,34,16,128]{3,2,1,0:T(8,128)} %latb_h.1, ...), custom_call_target="tpu_custom_call" | custom-call | tf_op jit(solution)/shard_map/pallas_call | solution.py:798
  17.3 0.8 %shard_map.114 = (f32[34,16,128]{2,1,0:T(8,128)}, f32[2,256]{1,0:T(2,128)}) custom-call(f32[34,16,128]{2,1,0:T(8,128)S(1)} %get-tuple-element.5.adjoint_v, f32[32,2,256]{2,1,0:T(2,128)S(1)} %get-tuple-element.6.land, f32[256,256]{1,0:T(8,128)S(1)} %get-tuple-element.7.cov), custom_call_target="tpu_custom_call" | custom-call | tf_op jit(solution)/shard_map/pallas_call | solution.py:823

commit v7 on v6

--- a/solution.py
+++ b/solution.py
@@ -442,8 +442,7 @@
             amat[...], cht[...], (((1,), (1,)), ((), ())), preferred_element_type=jnp.float32
         )
         sums = sums[:many] + sums[many:]
-        for group in range(many // 2):
-            send_ref[group] = sums[2 * group : 2 * group + 2]
+        send_ref[...] = sums
 
     tall_rows = rows + 2 * OWN
     few = slice(OWN - 2, OWN + rows + 6)
@@ -608,7 +607,7 @@
     def scatter(k, carry):
         device = lax.rem(me + k, count)
         pltpu.make_async_remote_copy(
-            src_ref=send_ref.at[group_of(device)],
+            src_ref=send_ref.at[pl.ds(2 * group_of(device), 2), :],
             dst_ref=land.at[me],
             send_sem=all_sem.at[0],
             recv_sem=all_sem.at[1],
@@ -690,7 +689,7 @@
     send_border(0, 1, 7)
     push_totals()
     lax.fori_loop(1, count, scatter, 0)
-    fetch(send_ref.at[group_of(me)], land.at[me], 5)
+    fetch(send_ref.at[pl.ds(2 * group_of(me), 2), :], land.at[me], 5)
     lat_inner(0)
     drain(recv_sem.at[0], lon_rows)
     drain_beside(recv_sem.at[8], 3 * rows)
@@ -788,7 +787,7 @@
         vm((2 * (regions // blk), (rows + 5) * lanes), b16),
         vm((blk, (rows + 5) * lanes), b16),
         vm((4 * (regions // blk), (rows + 5) * lanes), b16),
-        vm((regions // blk, 2, blk), f32),
+        vm((2 * (regions // blk), blk), f32),
         vm((5 * levels * rows, lanes), f32),
         pltpu.SemaphoreType.DMA((6,)),
         pltpu.SemaphoreType.DMA((2,)),

time: 18.2 us -> 18.2 us (level)
  no operation moved by 1% of the time
where the time goes in v7:
time: 18.2 us; the launch traced here: 18.1 us
  Pallas kernels  17.4 us (96%)
  between operations  0.64 us (4%)
    pallas_call x1, Pallas kernels, per_device(): pl.pallas_call(functools.partial(kernel, nlon, nlat, width), out_shape=(p...  16.6 us
    pallas_call x1, Pallas kernels, per_device(): pl.pallas_call(finish, out_shape=(jax.ShapeDtypeStruct(field, f32), jax.S...  0.79 us

profile of v7, /device:TPU:0, one launch (start us, length us, event | category | flops | bytes accessed | tf_op | source)
XLA Modules:
  0.0 18.1 jit_solution(16960661590821013967)
XLA Ops:
  0.6 16.6 %shard_map.113 = (f32[34,16,128]{2,1,0:T(8,128)S(1)}, f32[32,2,256]{2,1,0:T(2,128)S(1)}, f32[256,256]{1,0:T(8,128)S(1)}) custom-call(f32[34,16,128]{2,1,0:T(8,128)} %adj_h.1, f32[2,34,16,128]{3,2,1,0:T(8,128)} %lonc_h.1, s32[2,34,16,128]{3,2,1,0:T(8,128)} %lonb_h.1, f32[2,34,16,128]{3,2,1,0:T(8,128)} %latc_h.1, s32[2,34,16,128]{3,2,1,0:T(8,128)} %latb_h.1, ...), custom_call_target="tpu_custom_call" | custom-call | tf_op jit(solution)/shard_map/pallas_call | solution.py:797
  17.3 0.8 %shard_map.114 = (f32[34,16,128]{2,1,0:T(8,128)}, f32[2,256]{1,0:T(2,128)}) custom-call(f32[34,16,128]{2,1,0:T(8,128)S(1)} %get-tuple-element.5.adjoint_v, f32[32,2,256]{2,1,0:T(2,128)S(1)} %get-tuple-element.6.land, f32[256,256]{1,0:T(8,128)S(1)} %get-tuple-element.7.cov), custom_call_target="tpu_custom_call" | custom-call | tf_op jit(solution)/shard_map/pallas_call | solution.py:822
